TPU v7x, 128 devices: a whole 4x4x4 slice. The times are simulated.
128 devices in a mesh: batch: 8 (over z, core), seq: 16 (over x, y).
Axes of the slice: x: 4, y: 4, z: 4, core: 2. Of those that a mesh axis runs over, the one named last changes fastest.
Arguments:
- tokens: bfloat16 [16384, 2048], P(('batch', 'seq')), may hold values from -6 to 6
- lengths: int32 [8, 3], P('batch'), may hold values from 1 to 2046, as said below
- attn_gain: bfloat16 [2048], P(('batch', 'seq')), may hold values from 0.5 to 1.5
- w_query: bfloat16 [2048, 2048], P(('batch', 'seq')), may hold values from -0.125 to 0.125
- w_key: bfloat16 [2048, 256], P(('batch', 'seq')), may hold values from -0.125 to 0.125
- w_value: bfloat16 [2048, 256], P(('batch', 'seq')), may hold values from -0.125 to 0.125
- w_out: bfloat16 [2048, 2048], P(('batch', 'seq')), may hold values from -2 to 2
- mlp_gain: bfloat16 [2048], P(('batch', 'seq')), may hold values from 0.5 to 1.5
- w_gate: bfloat16 [2048, 5632], P(('batch', 'seq')), may hold values from -0.125 to 0.125
- w_up: bfloat16 [2048, 5632], P(('batch', 'seq')), may hold values from -0.125 to 0.125
- w_down: bfloat16 [5632, 2048], P(('batch', 'seq')), may hold values from -0.078125 to 0.078125
- cotangent: bfloat16 [16384, 2048], P(('batch', 'seq')), may hold values from -6 to 6
Outputs:
- output: bfloat16 [16384, 2048], P(('batch', 'seq'))
- grad_tokens: float32 [16384, 2048], P(('batch', 'seq'))
- grad_attn_gain: float32 [2048], P(('batch', 'seq'))
- grad_query: float32 [2048, 2048], P(('batch', 'seq'))
- grad_key: float32 [2048, 256], P(('batch', 'seq'))
- grad_value: float32 [2048, 256], P(('batch', 'seq'))
- grad_out: float32 [2048, 2048], P(('batch', 'seq'))
- grad_mlp_gain: float32 [2048], P(('batch', 'seq'))
- grad_gate: float32 [2048, 5632], P(('batch', 'seq'))
- grad_up: float32 [2048, 5632], P(('batch', 'seq'))
- grad_down: float32 [5632, 2048], P(('batch', 'seq'))
Inputs may be any that keep to these rules, and one draw needn't show every extreme that they name: Row g lists in order the lengths of the three documents packed into the 2048 tokens of group g; they sum to 2048; the first and the last are shorter than 128.
All inputs are finite; a program needn't handle non-finite values.
Results may differ from a plain program's by a relative error of at most 0.015.
Values may be sent and summed in bfloat16 or wider, within the bound.
A program may use at most 448 MiB of HBM per device.

v0:
```python
import math

import jax
import jax.numpy as jnp
from jax import lax
from jax.sharding import PartitionSpec as P

HEADS = 32
KV_HEADS = 4
HEAD_DIM = 64


EPS = 1e-05
THETA = 10000.0


def left_dot(left_arg, right_arg):
    return lax.dot_general(
        left_arg, right_arg, (((0,), (0,)), ((), ())), preferred_element_type=jnp.float32
    )


def right_dot(left_arg, right_arg):
    return lax.dot_general(
        left_arg, right_arg, (((1,), (1,)), ((), ())), preferred_element_type=jnp.float32
    )


def plain_dot(left_arg, right_arg):
    return jnp.dot(left_arg, right_arg, preferred_element_type=jnp.float32)


def doc_layout(lengths_row, positions):
    first_end = lengths_row[0]
    second_end = lengths_row[0] + lengths_row[1]
    segment = (positions >= first_end).astype(jnp.int32) + (positions >= second_end).astype(
        jnp.int32
    )
    doc_start = jnp.where(segment == 0, 0, jnp.where(segment == 1, first_end, second_end))
    return (segment, positions - doc_start)


def rotary_tables(offsets):
    half_dim = HEAD_DIM // 2
    frequency = jnp.exp(
        jnp.arange(half_dim, dtype=jnp.float32) * (-2.0 * math.log(THETA) / HEAD_DIM)
    )
    angles = offsets.astype(jnp.float32)[:, None] * frequency[None, :]
    angles = jnp.concatenate([angles, angles], axis=1)
    return (jnp.cos(angles), jnp.sin(angles))


def rotate(values, cosine_table, sine_table, head_count):
    row_count = values.shape[0]
    shaped = values.reshape(row_count, head_count, HEAD_DIM)
    half_dim = HEAD_DIM // 2
    turned = jnp.concatenate([-shaped[..., half_dim:], shaped[..., :half_dim]], axis=-1)
    result = shaped * cosine_table[:, None, :] + turned * sine_table[:, None, :]
    return result.reshape(row_count, head_count * HEAD_DIM)


def rotate_back(values, cosine_table, sine_table, head_count):
    row_count = values.shape[0]
    shaped = values.reshape(row_count, head_count, HEAD_DIM)
    half_dim = HEAD_DIM // 2
    scaled = shaped * sine_table[:, None, :]
    turned = jnp.concatenate([scaled[..., half_dim:], -scaled[..., :half_dim]], axis=-1)
    result = shaped * cosine_table[:, None, :] + turned
    return result.reshape(row_count, head_count * HEAD_DIM)


def local(
    tokens,
    lengths,
    attn_gain,
    w_query,
    w_key,
    w_value,
    w_out,
    mlp_gain,
    w_gate,
    w_up,
    w_down,
    cotangent,
):
    seq_devices = lax.axis_size("seq")
    tok_rows = tokens.shape[0]
    seq_rows = tok_rows * seq_devices
    own_heads = HEADS // seq_devices
    copies = HEADS
    own_copies = copies // seq_devices
    group_size = own_heads // own_copies
    block_rows = min(512, seq_rows)
    blocks = seq_rows // block_rows
    score_scale = HEAD_DIM ** (-0.5)
    attn_set = (
        lax.all_gather(attn_gain, ("batch", "seq"), axis=0, tiled=True),
        lax.all_gather(w_query, ("batch", "seq"), axis=0, tiled=True),
        lax.all_gather(w_key, ("batch", "seq"), axis=0, tiled=True),
        lax.all_gather(w_value, ("batch", "seq"), axis=0, tiled=True),
        lax.all_gather(w_out, ("batch", "seq"), axis=0, tiled=True),
    )
    all_positions = jnp.arange(seq_rows, dtype=jnp.int32)
    segment_all, offset_all = doc_layout(lengths[0], all_positions)
    own_offsets = lax.dynamic_slice_in_dim(
        offset_all, lax.axis_index("seq") * tok_rows, tok_rows, 0
    )
    cosine_table, sine_table = rotary_tables(own_offsets)
    inputs = tokens.astype(jnp.float32)
    recip_one = lax.rsqrt(jnp.mean(inputs * inputs, axis=1, keepdims=True) + EPS)
    normed_one = (inputs * recip_one * attn_set[0].astype(jnp.float32)).astype(jnp.bfloat16)
    query_rot = rotate(plain_dot(normed_one, attn_set[1]), cosine_table, sine_table, HEADS).astype(
        jnp.bfloat16
    )
    key_rot = rotate(plain_dot(normed_one, attn_set[2]), cosine_table, sine_table, KV_HEADS).astype(
        jnp.bfloat16
    )
    value_low = plain_dot(normed_one, attn_set[3]).astype(jnp.bfloat16)
    key_copy = jnp.repeat(
        key_rot.reshape(tok_rows, KV_HEADS, HEAD_DIM), copies // KV_HEADS, axis=1
    ).reshape(tok_rows, copies * HEAD_DIM)
    value_copy = jnp.repeat(
        value_low.reshape(tok_rows, KV_HEADS, HEAD_DIM), copies // KV_HEADS, axis=1
    ).reshape(tok_rows, copies * HEAD_DIM)
    query_heads, key_heads, value_heads = (
        lax.all_to_all(query_rot, "seq", split_axis=1, concat_axis=0, tiled=True),
        lax.all_to_all(key_copy, "seq", split_axis=1, concat_axis=0, tiled=True),
        lax.all_to_all(value_copy, "seq", split_axis=1, concat_axis=0, tiled=True),
    )
    query_four = query_heads.reshape(seq_rows, own_copies, group_size, HEAD_DIM)
    key_three = key_heads.reshape(seq_rows, own_copies, HEAD_DIM)
    value_three = value_heads.reshape(seq_rows, own_copies, HEAD_DIM)

    def block_scores(block_index):
        row_start = block_index * block_rows
        query_block = lax.dynamic_slice_in_dim(query_four, row_start, block_rows, 0)
        scores = (
            jnp.einsum("qcrd,kcd->crqk", query_block, key_three, preferred_element_type=jnp.float32)
            * score_scale
        )
        rows_seg = lax.dynamic_slice_in_dim(segment_all, row_start, block_rows, 0)
        rows_pos = row_start + jnp.arange(block_rows, dtype=jnp.int32)
        allowed = (rows_seg[:, None] == segment_all[None, :]) & (
            all_positions[None, :] <= rows_pos[:, None]
        )
        return (jnp.where(allowed[None, None], scores, -1e30), query_block)

    def forward_block(block_index):
        scores, query_block = block_scores(block_index)
        log_total = jax.nn.logsumexp(scores, axis=-1)
        weights_low = jnp.exp(scores - log_total[..., None]).astype(jnp.bfloat16)
        attended = jnp.einsum(
            "crqk,kcd->qcrd", weights_low, value_three, preferred_element_type=jnp.float32
        )
        return (attended.reshape(block_rows, own_heads * HEAD_DIM), log_total)

    attended, log_totals = lax.map(forward_block, jnp.arange(blocks, dtype=jnp.int32))
    attended = attended.reshape(seq_rows, own_heads * HEAD_DIM).astype(jnp.bfloat16)
    mixed_heads = lax.all_to_all(attended, "seq", split_axis=0, concat_axis=1, tiled=True)
    hidden = inputs + plain_dot(mixed_heads, attn_set[4])
    mlp_set = (
        lax.all_gather(mlp_gain, ("batch", "seq"), axis=0, tiled=True),
        lax.all_gather(w_gate, ("batch", "seq"), axis=0, tiled=True),
        lax.all_gather(w_up, ("batch", "seq"), axis=0, tiled=True),
        lax.all_gather(w_down, ("batch", "seq"), axis=0, tiled=True),
    )
    recip_two = lax.rsqrt(jnp.mean(hidden * hidden, axis=1, keepdims=True) + EPS)
    normed_two = (hidden * recip_two * mlp_set[0].astype(jnp.float32)).astype(jnp.bfloat16)
    gate_pre = plain_dot(normed_two, mlp_set[1])
    upward = plain_dot(normed_two, mlp_set[2])
    gate_sig = jax.nn.sigmoid(gate_pre)
    gate_act = gate_pre * gate_sig
    activated = (gate_act * upward).astype(jnp.bfloat16)
    output = (hidden + plain_dot(activated, mlp_set[3])).astype(jnp.bfloat16)
    mlp_back = (
        lax.all_gather(mlp_gain, ("batch", "seq"), axis=0, tiled=True),
        lax.all_gather(w_gate, ("batch", "seq"), axis=0, tiled=True),
        lax.all_gather(w_up, ("batch", "seq"), axis=0, tiled=True),
        lax.all_gather(w_down, ("batch", "seq"), axis=0, tiled=True),
    )
    grad_output = cotangent.astype(jnp.float32)
    grad_wdown = left_dot(activated, cotangent)
    grad_act = right_dot(cotangent, mlp_back[3])
    grad_gate_pre = (grad_act * upward * gate_sig * (1.0 + gate_pre * (1.0 - gate_sig))).astype(
        jnp.bfloat16
    )
    grad_upward = (grad_act * gate_act).astype(jnp.bfloat16)
    grad_wgate = left_dot(normed_two, grad_gate_pre)
    grad_wup = left_dot(normed_two, grad_upward)
    grad_normed_two = right_dot(grad_gate_pre, mlp_back[1]) + right_dot(grad_upward, mlp_back[2])
    grad_gain_two = jnp.sum(grad_normed_two * hidden * recip_two, axis=0)
    scaled_two = grad_normed_two * mlp_back[0].astype(jnp.float32)
    grad_hidden = (
        grad_output
        + recip_two * scaled_two
        - hidden * recip_two**3 * jnp.mean(scaled_two * hidden, axis=1, keepdims=True)
    )
    mlp_grads = (
        lax.psum_scatter(grad_gain_two, ("batch", "seq"), scatter_dimension=0, tiled=True),
        lax.psum_scatter(grad_wgate, ("batch", "seq"), scatter_dimension=0, tiled=True),
        lax.psum_scatter(grad_wup, ("batch", "seq"), scatter_dimension=0, tiled=True),
        lax.psum_scatter(grad_wdown, ("batch", "seq"), scatter_dimension=0, tiled=True),
    )
    attn_back = (
        lax.all_gather(attn_gain, ("batch", "seq"), axis=0, tiled=True),
        lax.all_gather(w_query, ("batch", "seq"), axis=0, tiled=True),
        lax.all_gather(w_key, ("batch", "seq"), axis=0, tiled=True),
        lax.all_gather(w_value, ("batch", "seq"), axis=0, tiled=True),
        lax.all_gather(w_out, ("batch", "seq"), axis=0, tiled=True),
    )
    grad_attn = grad_hidden.astype(jnp.bfloat16)
    grad_wout = left_dot(mixed_heads, grad_attn)
    grad_mixed = right_dot(grad_attn, attn_back[4]).astype(jnp.bfloat16)
    grad_heads = lax.all_to_all(grad_mixed, "seq", split_axis=1, concat_axis=0, tiled=True)
    grad_four = grad_heads.reshape(seq_rows, own_copies, group_size, HEAD_DIM)

    def backward_block(running, block_index):
        key_sum, value_sum = running
        scores, query_block = block_scores(block_index)
        grad_block = lax.dynamic_slice_in_dim(grad_four, block_index * block_rows, block_rows, 0)
        soft_weights = jnp.exp(scores - log_totals[block_index][..., None])
        grad_soft = jnp.einsum(
            "qcrd,kcd->crqk", grad_block, value_three, preferred_element_type=jnp.float32
        )
        row_inner = jnp.sum(soft_weights * grad_soft, axis=-1, keepdims=True)
        grad_scores = (soft_weights * (grad_soft - row_inner)).astype(jnp.bfloat16)
        grad_query_block = (
            jnp.einsum("crqk,kcd->qcrd", grad_scores, key_three, preferred_element_type=jnp.float32)
            * score_scale
        )
        key_sum = (
            key_sum
            + jnp.einsum(
                "crqk,qcrd->kcd", grad_scores, query_block, preferred_element_type=jnp.float32
            )
            * score_scale
        )
        value_sum = value_sum + jnp.einsum(
            "crqk,qcrd->kcd",
            soft_weights.astype(jnp.bfloat16),
            grad_block,
            preferred_element_type=jnp.float32,
        )
        return ((key_sum, value_sum), grad_query_block.reshape(block_rows, own_heads * HEAD_DIM))

    zero_grad = jnp.zeros((seq_rows, own_copies, HEAD_DIM), jnp.float32)
    (key_grad, value_grad), query_grad = lax.scan(
        backward_block, (zero_grad, zero_grad), jnp.arange(blocks, dtype=jnp.int32)
    )
    query_back, key_back, value_back = (
        lax.all_to_all(
            query_grad.reshape(seq_rows, own_heads * HEAD_DIM).astype(jnp.bfloat16),
            "seq",
            split_axis=0,
            concat_axis=1,
            tiled=True,
        ).astype(jnp.float32),
        lax.all_to_all(
            key_grad.reshape(seq_rows, own_copies * HEAD_DIM).astype(jnp.bfloat16),
            "seq",
            split_axis=0,
            concat_axis=1,
            tiled=True,
        ).astype(jnp.float32),
        lax.all_to_all(
            value_grad.reshape(seq_rows, own_copies * HEAD_DIM).astype(jnp.bfloat16),
            "seq",
            split_axis=0,
            concat_axis=1,
            tiled=True,
        ).astype(jnp.float32),
    )
    key_back = jnp.sum(
        key_back.reshape(tok_rows, KV_HEADS, copies // KV_HEADS, HEAD_DIM), axis=2
    ).reshape(tok_rows, KV_HEADS * HEAD_DIM)
    value_back = jnp.sum(
        value_back.reshape(tok_rows, KV_HEADS, copies // KV_HEADS, HEAD_DIM), axis=2
    ).reshape(tok_rows, KV_HEADS * HEAD_DIM)
    grad_query_pre = rotate_back(query_back, cosine_table, sine_table, HEADS).astype(jnp.bfloat16)
    grad_key_pre = rotate_back(key_back, cosine_table, sine_table, KV_HEADS).astype(jnp.bfloat16)
    grad_value_pre = value_back.astype(jnp.bfloat16)
    grad_wquery = left_dot(normed_one, grad_query_pre)
    grad_wkey = left_dot(normed_one, grad_key_pre)
    grad_wvalue = left_dot(normed_one, grad_value_pre)
    grad_normed_one = (
        right_dot(grad_query_pre, attn_back[1])
        + right_dot(grad_key_pre, attn_back[2])
        + right_dot(grad_value_pre, attn_back[3])
    )
    grad_gain_one = jnp.sum(grad_normed_one * inputs * recip_one, axis=0)
    scaled_one = grad_normed_one * attn_back[0].astype(jnp.float32)
    grad_inputs = (
        grad_hidden
        + recip_one * scaled_one
        - inputs * recip_one**3 * jnp.mean(scaled_one * inputs, axis=1, keepdims=True)
    )
    attn_grads = (
        lax.psum_scatter(grad_gain_one, ("batch", "seq"), scatter_dimension=0, tiled=True),
        lax.psum_scatter(grad_wquery, ("batch", "seq"), scatter_dimension=0, tiled=True),
        lax.psum_scatter(grad_wkey, ("batch", "seq"), scatter_dimension=0, tiled=True),
        lax.psum_scatter(grad_wvalue, ("batch", "seq"), scatter_dimension=0, tiled=True),
        lax.psum_scatter(grad_wout, ("batch", "seq"), scatter_dimension=0, tiled=True),
    )
    return (
        output,
        grad_inputs,
        attn_grads[0],
        attn_grads[1],
        attn_grads[2],
        attn_grads[3],
        attn_grads[4],
        mlp_grads[0],
        mlp_grads[1],
        mlp_grads[2],
        mlp_grads[3],
    )


def solution(mesh):
    in_specs = (
        P(("batch", "seq"), None),
        P("batch", None),
        P(("batch", "seq")),
        P(("batch", "seq"), None),
        P(("batch", "seq"), None),
        P(("batch", "seq"), None),
        P(("batch", "seq"), None),
        P(("batch", "seq")),
        P(("batch", "seq"), None),
        P(("batch", "seq"), None),
        P(("batch", "seq"), None),
        P(("batch", "seq"), None),
    )
    out_specs = (
        P(("batch", "seq"), None),
        P(("batch", "seq"), None),
        P(("batch", "seq")),
        P(("batch", "seq"), None),
        P(("batch", "seq"), None),
        P(("batch", "seq"), None),
        P(("batch", "seq"), None),
        P(("batch", "seq")),
        P(("batch", "seq"), None),
        P(("batch", "seq"), None),
        P(("batch", "seq"), None),
    )
    return jax.shard_map(local, mesh=mesh, in_specs=in_specs, out_specs=out_specs, check_vma=False)
```

profile of v0, /device:TPU:1, one launch (start us, length us, event | category | flops | bytes accessed | tf_op | source)
XLA Modules:
  0.0 4877.2 jit_solution(9150372734365438209)
XLA Ops:
  13.6 69.7 %all-reduce.7 = (bf16[2048]{0:T(1024)(128)(2,1)S(1)}, bf16[2048]{0:T(1024)(128)(2,1)S(1)}) all-reduce(bf16[2048]{0:T(1024)(128)(2,1)S(1)} %dynamic-update-slice, bf16[2048]{0:T(1024)(128)(2,1)S(1)} %dynamic-update-slice.1), channel_id=1, replica_groups=mesh['batch'=8,'seq'=16] {'batch','seq'}, use_global_device_ids=true, to_apply=%add | all-reduce | flops 4096 | bytes 16384
  92.1 49.8 %all-gather.11.cloned.1.call-done = bf16[2048,256]{1,0:T(8,128)(2,1)} async-done(((bf16[16,256]{1,0:T(8,128)(2,1)}), bf16[2048,256]{1,0:T(8,128)(2,1)}) %all-gather.11.cloned.1.call-update) | async-done | bytes 1048592 | tf_op jit(solution)/shard_map/all_gather | solution.py:99
  145.0 4.2 all-to-all-start.1
  149.1 63.9 %all-gather.9.cloned.1.call-done = bf16[2048,2048]{1,0:T(8,128)(2,1)} async-done(((bf16[16,2048]{1,0:T(8,128)(2,1)}), bf16[2048,2048]{1,0:T(8,128)(2,1)}) %all-gather.9.cloned.1.call-update) | async-done | bytes 8388624 | tf_op jit(solution)/shard_map/all_gather | solution.py:98
  213.0 4.7 fusion.86
  222.2 4.2 all-to-all-start.2
  233.5 3.5 all-to-all-done.2
  237.0 4.5 all-to-all-start
  243.7 6.8 all-to-all-done
  252.8 44.4 while.28
  255.3 2.9 fusion.167
  266.4 2.9 fusion.167
  277.6 2.9 fusion.167
  288.7 2.9 fusion.167
  297.2 5.1 all-to-all-start.3
  302.3 9.6 all-to-all-done.3
  312.3 4.9 multiply_reduce_fusion.2
  317.4 65.0 %all-gather.21.cloned.1.call-done = bf16[128,44,2048]{2,1,0:T(8,128)(2,1)} async-done(((bf16[1,44,2048]{2,1,0:T(8,128)(2,1)}), bf16[128,44,2048]{2,1,0:T(8,128)(2,1)}) %all-gather.21.cloned.1.call-update) | async-done | bytes 23068688 | tf_op jit(solution)/shard_map/all_gather | solution.py:165
  382.4 30.2 reshape.461
  412.6 62.1 %all-gather.19.cloned.1.call-done = bf16[2048,5632]{1,0:T(8,128)(2,1)} async-done(((bf16[16,5632]{1,0:T(8,128)(2,1)}), bf16[2048,5632]{1,0:T(8,128)(2,1)}) %all-gather.19.cloned.1.call-update) | async-done | bytes 23068688 | tf_op jit(solution)/shard_map/all_gather | solution.py:164
  474.8 12.3 fusion.92
  487.1 80.2 %all-gather.17.cloned.1.call-done = bf16[2048,5632]{1,0:T(8,128)(2,1)} async-done(((bf16[16,5632]{1,0:T(8,128)(2,1)}), bf16[2048,5632]{1,0:T(8,128)(2,1)}) %all-gather.17.cloned.1.call-update) | async-done | bytes 23068688 | tf_op jit(solution)/shard_map/all_gather | solution.py:163
  567.3 12.3 fusion.91
  579.6 14.8 multiply_convert_fusion
  594.4 13.2 fusion.93
  607.6 13.1 multiply_reduce_fusion
  623.1 6.3 fusion.58
  630.4 6.5 all-to-all-start.4
  637.0 10.2 all-to-all-done.4
  649.5 88.4 %while.29 = (s32[]{:T(128)}, f32[2048,2,64]{0,2,1:T(8,128)S(1)}, f32[2048,2,64]{0,2,1:T(8,128)}, bf16[4,512,128]{2,1,0:T(8,128)(2,1)}, s32[4]{0:T(128)S(1)}, /*i...) while((s32[]{:T(128)}, f32[2048,2,64]{0,2,1:T(8,128)S(1)}, ...), condition=%wide.region_9.10_spmd.clone, body=%wide.region_7.9_spmd.clone.sunk | while | flops 1378221568 | bytes 74103080 | solution.py:247
  656.4 4.4 fusion.185
  660.8 4.1 fusion.182
  678.2 4.8 fusion.185
  683.0 4.1 fusion.182
  700.3 4.8 fusion.185
  705.1 4.1 fusion.182
  722.5 4.8 fusion.185
  727.3 4.1 fusion.182
  739.5 12.8 all_to_all.111
  754.7 12.9 all_to_all.112
  770.1 8.2 fusion.69
  779.3 12.5 all_to_all.110
  795.0 8.3 fusion.81
  804.3 19.2 fusion.96
  824.1 19.3 fusion.95
  844.7 18.9 fusion.97
  863.6 569.1 %fusion.4 = f32[48,2048]{1,0:T(8,128)S(1)} fusion(f32[5632,2048]{1,0:T(8,128)} %fusion.97), kind=kCustom, calls=%all-reduce-scatter | all-reduce-scatter fusion | flops 12582913 | bytes 46530560
  1439.2 3.5 collective-permute-start.7
  1442.8 4.9 collective-permute-start.6
  1447.6 2.7 collective-permute-done.10
  1452.3 9.4 collective-permute-done.9
  1464.1 24.8 collective-permute-start.3
  1492.8 3.3 collective-permute-start
  1496.1 12.0 fusion.57
  1509.9 7.9 collective-permute-done.1
  1518.5 5.5 collective-permute-done
  1524.0 30.9 concatenate.34
  1556.8 6.3 fusion.94
  1565.6 73.4 %all-reduce.6 = (f32[2048]{0:T(1024)S(1)}, f32[2048]{0:T(1024)S(1)}) all-reduce(f32[2048]{0:T(1024)S(1)} %get-tuple-element.205, f32[2048]{0:T(1024)S(1)} %copy-done.29), channel_id=2, replica_groups=mesh['batch'=8,'seq'=16] {'batch','seq'}, use_global_device_ids=true, to_apply=%region_14.15.clone | all-reduce | flops 4096 | bytes 32768
  1641.4 394.6 %reduce-scatter.11.cloned.1.call-done = f32[16,256]{1,0:T(8,128)} async-done(((f32[2048,256]{1,0:T(8,128)}), f32[16,256]{1,0:T(8,128)}) %reduce-scatter.11.cloned.1.call-update) | async-done | bytes 16400 | tf_op jit(solution)/shard_map/reduce_scatter | solution.py:300
  2036.0 677.8 %reduce-scatter.15.cloned.1.call-done = f32[16,2048]{1,0:T(8,128)} async-done(((f32[2048,2048]{1,0:T(8,128)}), f32[16,2048]{1,0:T(8,128)}) %reduce-scatter.15.cloned.1.call-update) | async-done | bytes 131088 | tf_op jit(solution)/shard_map/reduce_scatter | solution.py:302
  2713.8 673.7 %reduce-scatter.9.cloned.1.call-done = f32[16,2048]{1,0:T(8,128)} async-done(((f32[2048,2048]{1,0:T(8,128)}), f32[16,2048]{1,0:T(8,128)}) %reduce-scatter.9.cloned.1.call-update) | async-done | bytes 131088 | tf_op jit(solution)/shard_map/reduce_scatter | solution.py:299
  3387.5 739.8 %reduce-scatter.19.cloned.1.call-done = f32[16,5632]{1,0:T(8,128)} async-done(((f32[2048,5632]{1,0:T(8,128)}), f32[16,5632]{1,0:T(8,128)}) %reduce-scatter.19.cloned.1.call-update) | async-done | bytes 360464 | tf_op jit(solution)/shard_map/reduce_scatter | solution.py:201
  4127.3 743.2 %reduce-scatter.17.cloned.1.call-done = f32[16,5632]{1,0:T(8,128)} async-done(((f32[2048,5632]{1,0:T(8,128)}), f32[16,5632]{1,0:T(8,128)}) %reduce-scatter.17.cloned.1.call-update) | async-done | bytes 360464 | tf_op jit(solution)/shard_map/reduce_scatter | solution.py:200
  (278 shorter events, 148.6 us)
Async XLA Ops:
  7.2 205.8 %copy-start = (bf16[128,2048]{1,0:T(8,128)(2,1)S(1)}, bf16[128,2048]{1,0:T(8,128)(2,1)}, u32[]{:S(2)}) copy-start(bf16[128,2048]{1,0:T(8,128)(2,1)} %param.16) | copy-start | bytes 1572868
  7.2 83.0 %all-gather.13.cloned.1.call-start = ((), (), s32[]{:S(2)}) async-start(), calls=%async_computation.16 | async-start | bytes 1056768 | tf_op jit(solution)/shard_map/all_gather | solution.py:100
  7.9 134.0 %all-gather.11.cloned.1.call-start = ((), (), s32[]{:S(2)}) async-start(), calls=%async_computation.15 | async-start | bytes 1056768 | tf_op jit(solution)/shard_map/all_gather | solution.py:99
  8.7 204.3 %all-gather.9.cloned.1.call-start = ((), (), s32[]{:S(2)}) async-start(), calls=%async_computation.14 | async-start | bytes 8454144 | tf_op jit(solution)/shard_map/all_gather | solution.py:98
  9.4 302.8 %all-gather.15.cloned.1.call-start = ((), (), s32[]{:S(2)}) async-start(), calls=%async_computation.17 | async-start | bytes 8454144 | tf_op jit(solution)/shard_map/all_gather | solution.py:101
  10.0 372.4 %all-gather.21.cloned.1.call-start = ((), (), s32[]{:S(2)}) async-start(), calls=%async_computation.26 | async-start | bytes 25362432 | tf_op jit(solution)/shard_map/all_gather | solution.py:165
  10.6 464.2 %all-gather.19.cloned.1.call-start = ((), (), s32[]{:S(2)}) async-start(), calls=%async_computation.19 | async-start | bytes 23248896 | tf_op jit(solution)/shard_map/all_gather | solution.py:164
  11.1 556.1 %all-gather.17.cloned.1.call-start = ((), (), s32[]{:S(2)}) async-start(), calls=%async_computation.18 | async-start | bytes 23248896 | tf_op jit(solution)/shard_map/all_gather | solution.py:163
  83.3 134.4 %copy-start.21 = (f32[2048]{0:T(1024)}, f32[2048]{0:T(1024)S(1)}, u32[]{:S(2)}) copy-start(f32[2048]{0:T(1024)S(1)} %convert_element_type.145) | copy-start | bytes 24580
  87.5 0.6 copy-start.19
  87.5 139.0 %copy-start.17 = (f32[128,64]{0,1:T(8,128)}, f32[128,64]{0,1:T(8,128)S(1)}, u32[]{:S(2)}) copy-start(f32[128,64]{0,1:T(8,128)S(1)} %get-tuple-element.265) | copy-start | bytes 98308
  90.2 127.5 %copy-start.27 = (f32[128]{0:T(128)}, f32[128]{0:T(128)S(1)}, u32[]{:S(2)}) copy-start(f32[128]{0:T(128)S(1)} %get-tuple-element.267) | copy-start | bytes 1540
  145.0 76.3 %all-to-all-start.1 = ((bf16[128,16,128]{0,2,1:T(8,128)(2,1)}), bf16[128,16,128]{0,2,1:T(8,128)(2,1)S(1)}, u32[]{:S(2)}, u32[]{:S(2)}) async-start(bf16[128,16,128]{0,2,1:T(8,128)(2,1)} %bitcast.10), calls=%async_computation.1 | async-start | bytes 1048576 | tf_op jit(solution)/shard_map/all_to_all | solution.py:127
  222.2 14.8 all-to-all-start.2
  237.0 13.5 all-to-all-start
  297.2 14.7 all-to-all-start.3
  312.2 5.0 copy-start.10
  317.2 303.6 %copy-start.2 = (f32[128,2048]{1,0:T(8,128)}, f32[128,2048]{1,0:T(8,128)S(1)}, u32[]{:S(2)}) copy-start(f32[128,2048]{1,0:T(8,128)S(1)} %get-tuple-element.273) | copy-start | bytes 3145732
  317.4 249.9 %copy-start.6 = (bf16[128,2048]{1,0:T(8,128)(2,1)}, bf16[128,2048]{1,0:T(8,128)(2,1)S(1)}, u32[]{:S(2)}) copy-start(bf16[128,2048]{1,0:T(8,128)(2,1)S(1)} %multiply_convert_fusion.3) | copy-start | bytes 1572868
  487.1 92.5 %copy-start.14 = (bf16[128,2048]{1,0:T(8,128)(2,1)S(1)}, bf16[128,2048]{1,0:T(8,128)(2,1)}, u32[]{:S(2)}) copy-start(bf16[128,2048]{1,0:T(8,128)(2,1)} %param.27) | copy-start | bytes 1572868
  594.4 13.2 copy-start.8
  622.2 1.0 copy-start.4
  630.4 16.8 all-to-all-start.4
  636.9 1004.5 %reduce-scatter.13.cloned.1.call-start = ((), (), s32[]{:S(2)}) async-start(), calls=%async_computation.22 | async-start | bytes 2113536 | tf_op jit(solution)/shard_map/reduce_scatter | solution.py:301
  649.5 102.8 %copy-start.1 = (bf16[128,2048]{1,0:T(8,128)(2,1)S(1)}, bf16[128,2048]{1,0:T(8,128)(2,1)}, u32[]{:S(2)}) copy-start(bf16[128,2048]{1,0:T(8,128)(2,1)} %param.16) | copy-start | bytes 1572868
  649.5 102.9 %copy-start.22 = (f32[2048]{0:T(1024)S(1)}, f32[2048]{0:T(1024)}, u32[]{:S(2)}) copy-start(f32[2048]{0:T(1024)} %copy-done.21) | copy-start | bytes 24580
  649.5 102.9 %copy-start.28 = (f32[128]{0:T(128)S(1)}, f32[128]{0:T(128)}, u32[]{:S(2)}) copy-start(f32[128]{0:T(128)} %copy-done.27) | copy-start | bytes 1540
  739.2 28.6 copy-start.18
  739.3 28.6 copy-start.20
  754.3 15.9 copy-start.5
  754.3 15.9 copy-start.11
  754.3 1281.7 %reduce-scatter.11.cloned.1.call-start = ((), (), s32[]{:S(2)}) async-start(), calls=%async_computation.21 | async-start | bytes 2113536 | tf_op jit(solution)/shard_map/reduce_scatter | solution.py:300
  769.8 1944.0 %reduce-scatter.15.cloned.1.call-start = ((), (), s32[]{:S(2)}) async-start(), calls=%async_computation.23 | async-start | bytes 16908288 | tf_op jit(solution)/shard_map/reduce_scatter | solution.py:302
  778.3 1.0 copy-start.15
  778.3 2609.2 %reduce-scatter.9.cloned.1.call-start = ((), (), s32[]{:S(2)}) async-start(), calls=%async_computation.20 | async-start | bytes 16908288 | tf_op jit(solution)/shard_map/reduce_scatter | solution.py:299
  795.0 8.3 copy-start.12
  803.3 1.0 copy-start.7
  803.3 3324.0 %reduce-scatter.19.cloned.1.call-start = ((), (), s32[]{:S(2)}) async-start(), calls=%async_computation.25 | async-start | bytes 46497792 | tf_op jit(solution)/shard_map/reduce_scatter | solution.py:201
  823.5 4047.0 %reduce-scatter.17.cloned.1.call-start = ((), (), s32[]{:S(2)}) async-start(), calls=%async_computation.24 | async-start | bytes 46497792 | tf_op jit(solution)/shard_map/reduce_scatter | solution.py:200
  843.3 1.4 copy-start.9
  863.6 632.5 %copy-start.3 = (f32[128,2048]{1,0:T(8,128)S(1)}, f32[128,2048]{1,0:T(8,128)}, u32[]{:S(2)}) copy-start(f32[128,2048]{1,0:T(8,128)} %copy-done.2) | copy-start | bytes 3145732
  1432.7 17.6 collective-permute-start.10
  1434.7 27.0 collective-permute-start.9
  1436.6 27.5 collective-permute-start.8
  1439.2 49.7 %collective-permute-start.7 = (f32[48,2048]{1,0:T(8,128)S(1)}, f32[48,2048]{1,0:T(8,128)}, u32[]{:S(2)}, u32[]{:S(2)}) collective-permute-start(f32[48,2048]{1,0:T(8,128)S(1)} %fusion.4), channel_id=1, source_target_pairs={{0,8},{1,9},{2,10},{3,11},{4,12},{5,13},{6,14},{7,15},{8,16},{9,17... | collective-permute-start | bytes 1179656
  1442.8 48.1 collective-permute-start.6
  1450.4 42.5 collective-permute-start.5
  1461.7 46.4 collective-permute-start.4
  1464.1 44.1 collective-permute-start.3
  1489.0 21.0 collective-permute-start.2
  1490.9 26.9 collective-permute-start.1
  1492.8 31.2 collective-permute-start
  1508.1 48.7 copy-start.13
  1508.1 9.6 copy-start.23
  1508.2 9.6 copy-start.24
  1509.9 7.9 copy-start.25
  1517.8 0.7 copy-start.26
  1554.9 10.0 copy-start.16
  1556.8 8.7 copy-start.29
  1556.8 83.3 %copy-start.30 = (f32[128]{0:T(128)S(1)}, f32[128]{0:T(128)}, u32[]{:S(2)}) copy-start(f32[128]{0:T(128)} %get-tuple-element.266) | copy-start | bytes 1540
Sparse Core Ops, SparseCore 0:
  10.8 67.1 all-gather.12
  80.8 61.0 all-gather.10
  145.1 67.9 all-gather.8
  216.0 70.4 all-gather.14
  289.4 92.9 all-gather.20
  385.4 89.3 all-gather.18
  477.9 89.3 all-gather.16
  754.4 624.3 reduce-scatter.12
  1381.8 654.1 reduce-scatter.10
  2038.8 674.9 reduce-scatter.14
  2716.8 670.6 reduce-scatter.8
  3390.3 736.9 reduce-scatter.18
  4130.3 740.1 reduce-scatter.16
where the time goes:
time: 4920 us; the launch traced here: 4880 us
  waiting for transfers between devices  3610 us (73%)
  blocking collectives  750 us (15%)
  matrix products  261 us (5%)
  local copies, waits for them, and re-layouts  101 us (2%)
  starting transfers between devices  76.4 us (2%)
    reduce_scatter x1, waiting for transfers between devices, local(): lax.psum_scatter(grad_wgate, ('batch', 'seq'), scatter_dimension=0, tiled...  743 us
    reduce_scatter x1, waiting for transfers between devices, local(): lax.psum_scatter(grad_wup, ('batch', 'seq'), scatter_dimension=0, tiled=T...  740 us
    unnamed x3, blocking collectives  712 us
    reduce_scatter x1, waiting for transfers between devices, local(): lax.psum_scatter(grad_wout, ('batch', 'seq'), scatter_dimension=0, tiled=...  678 us
    reduce_scatter x1, waiting for transfers between devices, local(): lax.psum_scatter(grad_wquery, ('batch', 'seq'), scatter_dimension=0, tile...  674 us
    reduce_scatter x1, waiting for transfers between devices, local(): lax.psum_scatter(grad_wkey, ('batch', 'seq'), scatter_dimension=0, tiled=...  395 us
  transfers between devices with their start and end apart: 29, of which 20 were waited for; matrix products, arithmetic and copies ran while one was open for 17% of the time, Pallas kernels for 0%

commit v1 on v0

v1 whole, which is shorter than its diff:
```python
import functools
import math

import jax
import jax.numpy as jnp
from jax import lax
from jax.experimental import pallas as pl
from jax.experimental.pallas import tpu as pltpu
from jax.sharding import Mesh
from jax.sharding import PartitionSpec as P

HEADS = 32
KV_HEADS = 4
HD = 64
EPS = 1e-05
THETA = 10000.0
NEG = -1e30
BF = jnp.bfloat16
F32 = jnp.float32
ANY = pl.ANY
VMEM = pltpu.VMEM
TP = ("x", "core")
DP = ("z", "y")
ALL = ("z", "core", "x", "y")


def tdot(a, b):
    return lax.dot_general(a, b, (((0,), (0,)), ((), ())), preferred_element_type=F32)


def dott(a, b):
    return lax.dot_general(a, b, (((1,), (1,)), ((), ())), preferred_element_type=F32)


def dot(a, b):
    return jnp.dot(a, b, preferred_element_type=F32)


class Wire:
    def __init__(self, ssem, rsem):
        self.ssem, self.rsem, self.sent = ssem, rsem, []

    def put(self, src, dst, k, to):
        cp = pltpu.make_async_remote_copy(
            src_ref=src, dst_ref=dst, send_sem=self.ssem.at[k], recv_sem=self.rsem.at[k],
            device_id=to, device_id_type=pl.DeviceIdType.MESH)
        cp.start()
        self.sent.append(cp)

    def got(self, dst, k, to):
        pltpu.make_async_remote_copy(
            src_ref=dst, dst_ref=dst, send_sem=self.ssem.at[k], recv_sem=self.rsem.at[k],
            device_id=to, device_id_type=pl.DeviceIdType.MESH).wait_recv()

    def drain(self):
        for cp in self.sent:
            cp.wait_send()


def greet(peers):
    barrier = pltpu.get_barrier_semaphore()
    for to in peers:
        pl.semaphore_signal(barrier, inc=1, device_id=to, device_id_type=pl.DeviceIdType.MESH)
    pl.semaphore_wait(barrier, len(peers))


def cx_ring():
    c, x = lax.axis_index("core"), lax.axis_index("x")
    right, left, opp = lax.rem(x + 1, 4), lax.rem(x + 3, 4), lax.rem(x + 2, 4)
    return c, x, right, left, opp, {"x": right}, {"x": left}, {"core": 1 - c}


def comm_params(cid, mb=None):
    kw = {} if mb is None else {"vmem_limit_bytes": mb << 20}
    return pltpu.CompilerParams(collective_id=cid, has_side_effects=True, **kw)


class Mail(Wire):
    def __init__(self, ssem, rsem):
        super().__init__(ssem, rsem)
        self.used = 0

    def new(self):
        self.used += 1
        return self.used - 1


def around(q):
    return lax.rem(q + 1, 4), lax.rem(q + 3, 4), lax.rem(q + 2, 4)


def ring(w, s, axis, q):
    right, left, opp = around(q)
    to_r, to_l = {axis: right}, {axis: left}
    k = [w.new() for _ in range(4)]
    w.put(s(q, None), s(q, None), k[0], to_r)
    w.put(s(q, None), s(q, None), k[1], to_l)
    yield
    w.got(s(left, None), k[0], to_l)
    w.put(s(left, 0), s(left, 0), k[2], to_r)
    w.got(s(right, None), k[1], to_r)
    w.put(s(right, 1), s(right, 1), k[3], to_l)
    yield
    w.got(s(opp, 0), k[2], to_l)
    w.got(s(opp, 1), k[3], to_r)


def col_flows(w, W, z, y):
    cut = lambda h: slice(None) if h is None else pl.ds(2 * h, 2)

    def first():
        yield from ring(w, lambda p, h: W.at[z, 0, cut(h), p], "y", y)
        yield from ring(w, lambda p, h: W.at[p, 0, cut(h)], "z", z)

    def second():
        yield from ring(w, lambda p, h: W.at[p, 1, cut(h), y], "z", z)
        yield from ring(w, lambda p, h: W.at[:, 1, cut(h), p], "y", y)

    return [first(), second()]


def row_flows(w, W, z, y):
    n = W.shape[-1] // 4
    cut = lambda b, h: pl.ds(2 * n * b, 2 * n) if h is None else pl.ds(2 * n * b + n * h, n)

    def first():
        yield from ring(w, lambda p, h: W.at[z, p, :, cut(0, h)], "y", y)
        yield from ring(w, lambda p, h: W.at[p, :, :, cut(0, h)], "z", z)

    def second():
        yield from ring(w, lambda p, h: W.at[p, y, :, cut(1, h)], "z", z)
        yield from ring(w, lambda p, h: W.at[:, p, :, cut(1, h)], "y", y)

    return [first(), second()]


def pump(flows):
    for f in flows:
        next(f, None)


def gather8(w, src, dst):
    c, x, right, left, opp, to_r, to_l, to_c = cx_ring()
    rows = dst.shape[2]
    lo, hi = pl.ds(0, rows // 2), pl.ds(rows // 2, rows // 2)
    k = [w.new() for _ in range(9)]
    w.put(src, dst.at[c, x], k[0], to_r)
    w.put(src, dst.at[c, x], k[1], to_l)
    w.put(src, dst.at[c, x], k[4], to_c)
    yield
    w.got(dst.at[c, left], k[0], to_l)
    w.put(dst.at[c, left, lo], dst.at[c, left, lo], k[2], to_r)
    w.put(dst.at[c, left], dst.at[c, left], k[5], to_c)
    w.got(dst.at[c, right], k[1], to_r)
    w.put(dst.at[c, right, hi], dst.at[c, right, hi], k[3], to_l)
    w.put(dst.at[c, right], dst.at[c, right], k[6], to_c)
    yield
    w.got(dst.at[c, opp, lo], k[2], to_l)
    w.put(dst.at[c, opp, lo], dst.at[c, opp, lo], k[7], to_c)
    w.got(dst.at[c, opp, hi], k[3], to_r)
    w.put(dst.at[c, opp, hi], dst.at[c, opp, hi], k[8], to_c)
    yield
    w.got(dst.at[1 - c, x], k[4], to_c)
    w.got(dst.at[1 - c, left], k[5], to_c)
    w.got(dst.at[1 - c, right], k[6], to_c)
    w.got(dst.at[1 - c, opp, lo], k[7], to_c)
    w.got(dst.at[1 - c, opp, hi], k[8], to_c)


def add_to(dst, other, r0, rows, step=16):
    @pl.loop(0, rows // step)
    def _(i):
        a = pl.ds(pl.multiple_of(r0 + i * step, step), step)
        b = pl.ds(pl.multiple_of(i * step, step), step)
        dst[a, :] = (dst[a, :].astype(F32) + other[b, :].astype(F32)).astype(dst.dtype)


def scatter8_core(w, p, core_r, state):
    c, x, right, left, opp, to_r, to_l, to_c = cx_ring()
    state["k"] = [w.new() for _ in range(4)]
    for i, xx in enumerate((opp, right, left, x)):
        w.put(p.at[1 - c, xx], core_r.at[i], state["k"][i], to_c)


def scatter8_ring(w, p, core_r, hop, fin, state):
    c, x, right, left, opp, to_r, to_l, to_c = cx_ring()
    rows = p.shape[2]
    half = rows // 2
    lo, hi = pl.ds(0, half), pl.ds(half, half)
    kc = state["k"]
    k = [w.new() for _ in range(6)]
    w.got(core_r.at[0], kc[0], to_c)
    add_to(p.at[c, opp], core_r.at[0], 0, rows)
    w.put(p.at[c, opp, lo], hop.at[0], k[0], to_r)
    w.put(p.at[c, opp, hi], hop.at[1], k[1], to_l)
    w.got(core_r.at[1], kc[1], to_c)
    add_to(p.at[c, right], core_r.at[1], 0, rows)
    w.put(p.at[c, right, hi], fin.at[0, hi], k[2], to_r)
    w.got(core_r.at[2], kc[2], to_c)
    add_to(p.at[c, left], core_r.at[2], 0, rows)
    w.put(p.at[c, left, lo], fin.at[1, lo], k[3], to_l)
    yield
    w.got(hop.at[0], k[0], to_l)
    add_to(p.at[c, right], hop.at[0], 0, half)
    w.put(p.at[c, right, lo], fin.at[0, lo], k[4], to_r)
    w.got(hop.at[1], k[1], to_r)
    add_to(p.at[c, left], hop.at[1], half, half)
    w.put(p.at[c, left, hi], fin.at[1, hi], k[5], to_l)
    yield
    w.got(core_r.at[3], kc[3], to_c)
    w.got(fin.at[0, hi], k[2], to_l)
    w.got(fin.at[1, lo], k[3], to_r)
    w.got(fin.at[0, lo], k[4], to_l)
    w.got(fin.at[1, hi], k[5], to_r)


def lanes(shape):
    return lax.broadcasted_iota(jnp.int32, shape, len(shape) - 1)


def swap_halves(u):
    first = lax.rem(lanes(u.shape), 64) < 32
    return jnp.where(first, pltpu.roll(u, 96, u.ndim - 1), pltpu.roll(u, 32, u.ndim - 1))


def entry(peers, extra=None):
    barrier = pltpu.get_barrier_semaphore()
    for to in peers:
        pl.semaphore_signal(barrier, inc=1, device_id=to, device_id_type=pl.DeviceIdType.MESH)
    if extra is None:
        pl.semaphore_wait(barrier, len(peers))
        return
    more, to = extra

    @pl.when(more)
    def _():
        pl.semaphore_signal(barrier, inc=1, device_id=to, device_id_type=pl.DeviceIdType.MESH)
        pl.semaphore_wait(barrier, len(peers) + 1)

    @pl.when(jnp.logical_not(more))
    def _():
        pl.semaphore_wait(barrier, len(peers))


def tp_peers(c, x):
    r = 2 * x + c
    out = []
    for k in range(1, 8):
        rr = lax.rem(r + k, 8)
        out.append((rr, {"x": rr // 2, "core": lax.rem(rr, 2)}))
    return out


def spread(w, src, W, z, c, x, y, local_sem):
    ks = [w.new() for _ in range(7)]
    for k, (rr, to) in zip(ks, tp_peers(c, x)):
        w.put(src.at[rr], W.at[z, c, x, y], k, to)
    own = pltpu.make_async_copy(src.at[2 * x + c], W.at[z, c, x, y], local_sem)
    own.start()
    yield
    r = 2 * x + c
    for i, k in enumerate(ks):
        rr = lax.rem(r + 7 - i, 8)
        w.got(W.at[z, lax.rem(rr, 2), rr // 2, y], k, {"x": rr // 2, "core": lax.rem(rr, 2)})
    own.wait()


def transpose_zx(w, src, dst_of, z, x, local_sem):
    k = w.new()
    to = {"z": x, "x": z}

    def far():
        return pltpu.make_async_remote_copy(
            src_ref=src, dst_ref=dst_of(x), send_sem=w.ssem.at[k], recv_sem=w.rsem.at[k],
            device_id=to, device_id_type=pl.DeviceIdType.MESH)

    def near():
        return pltpu.make_async_copy(src, dst_of(x), local_sem)

    @pl.when(z != x)
    def _():
        far().start()

    @pl.when(z == x)
    def _():
        near().start()

    yield

    @pl.when(z != x)
    def _():
        far().wait_send()
        w.got(dst_of(z), k, to)

    @pl.when(z == x)
    def _():
        near().wait()


def attend(q, keys, j, y, c1, c2):
    n = keys.shape[0]
    s = dott(q, keys)
    row = lax.broadcasted_iota(jnp.int32, (512, 1), 0)
    place = (4 * j + y) * 128 + lax.rem(row, 128)
    start = jnp.where(place >= c2, c2, jnp.where(place >= c1, c1, 0))
    at = lax.broadcasted_iota(jnp.int32, (512, n), 1)
    s = jnp.where((at >= start) & (at <= place), s, NEG)
    top = jnp.max(s, axis=1, keepdims=True)
    e = jnp.exp(s - top)
    total = jnp.sum(e, axis=1, keepdims=True)
    return dot(e.astype(BF), keys) / total, top + jnp.log(total)


def pair_heads(first, second, lower):
    low = lanes(first.shape) < 64
    if lower:
        return jnp.where(low, first, pltpu.roll(second, 64, 1))
    return jnp.where(low, pltpu.roll(first, 64, 1), second)


def m1_kernel(lens, x_ref, cos, sin, cot, qkv_s, out_s, gate_s, up_s, down_s,
              h, n2, n1_out, cg, qp, kv, o, lse, wqkv, wout, wgate, wup, wdown,
              n1, p, core_r, hop, fin, ssem, rsem, lsem):
    z, c, x, y = (lax.axis_index(a) for a in ALL)
    peers = [to for _, to in tp_peers(c, x)]
    for axis, q in (("y", y), ("z", z)):
        peers += [{axis: lax.rem(q + 1, 4)}, {axis: lax.rem(q + 3, 4)}]
    entry(peers, (z != x, {"z": x, "x": z}))
    w = Mail(ssem, rsem)

    sp_qkv = spread(w, qkv_s, wqkv, z, c, x, y, lsem.at[0])
    pump([sp_qkv])

    @pl.loop(0, 8)
    def _(i):
        rows = pl.ds(pl.multiple_of(i * 16, 16), 16)
        v = x_ref[rows, :].astype(F32)
        n1[c, x, rows, :] = (v * lax.rsqrt(jnp.mean(v * v, axis=1, keepdims=True) + EPS)).astype(BF)

    ag_n1 = gather8(w, n1.at[c, x], n1)
    pump([ag_n1])
    tr_out = transpose_zx(w, out_s, lambda zz: wout.at[zz, y], z, x, lsem.at[1])
    sp_gate = spread(w, gate_s, wgate, z, c, x, y, lsem.at[2])
    sp_up = spread(w, up_s, wup, z, c, x, y, lsem.at[3])
    tr_down = transpose_zx(w, down_s, lambda zz: wdown.at[zz, y], z, x, lsem.at[4])
    early = [tr_out, sp_gate, sp_up, tr_down]
    pump(early)
    pump([sp_qkv])
    fl_qkv = col_flows(w, wqkv, z, y)
    pump(fl_qkv)
    pump(early)
    fl_qkv_out = fl_qkv + row_flows(w, wout, z, y)
    pump(fl_qkv_out[2:])
    pump(fl_qkv_out)
    pump(fl_qkv_out)
    pump([ag_n1])
    fl_mlp = col_flows(w, wgate, z, y) + col_flows(w, wup, z, y) + row_flows(w, wdown, z, y)
    pump(fl_mlp)
    pump(fl_qkv_out)
    pump([ag_n1])
    pump(fl_qkv_out)
    pump([ag_n1])
    pump(fl_mlp)

    save_n1 = pltpu.make_async_copy(n1, n1_out, lsem.at[5])
    save_n1.start()
    own_cot = pltpu.make_async_copy(cot, cg.at[c, x], lsem.at[6])
    own_cot.start()
    ag_cot = gather8(w, cot, cg)
    pump([ag_cot])

    weights = wqkv[...].reshape(2048, 384)

    def project(g, keys_too):
        u = dot(n1[g].reshape(512, 2048), weights)
        cs, sn = cos[g], sin[g]
        for t in range(2):
            v = u[:, 128 * t: 128 * t + 128]
            v = (v * cs + swap_halves(v) * sn) * (HD ** -0.5)
            low = lanes(v.shape) < 64
            for b, head in enumerate((v, pltpu.roll(v, 64, 1))):
                rows = pl.ds(128 * (2 * t + b), 128)
                qp[g, :, rows, :] = jnp.where(low, head, 0.0).astype(BF).reshape(4, 128, 128)
        if keys_too:
            v = u[:, 256:384]
            turned = jnp.where(lanes(v.shape) < 64, v * cs + swap_halves(v) * sn, v)
            kv[g, :, y] = turned.astype(BF).reshape(4, 128, 128)

    g0, g1 = 1 - c, c
    to_c = {"core": 1 - c}
    project(g0, True)
    halves = lambda h: slice(None) if h is None else pl.ds(2 * h, 2)
    fl_kv = [ring(w, lambda pp, hh: kv.at[g0, halves(hh), pp], "y", y)]
    pump(fl_kv)
    project(g1, False)
    pump(fl_mlp)
    pump(fl_kv)
    pump(fl_kv)
    k_kv = w.new()
    w.put(kv.at[g0], kv.at[g0], k_kv, to_c)

    state = {}
    out_w = wout[...].reshape(256, 2048)
    for turn_no, g in enumerate((g0, g1)):
        if turn_no == 1:
            w.got(kv.at[g], k_kv, to_c)
        for j in range(4):
            n = 512 * (j + 1)
            keys = kv[g, 0:j + 1].reshape(n, 128)
            res, total = attend(qp[g, j], keys, j, y, lens[g, 0], lens[g, 1])
            heads = [res[128 * a: 128 * a + 128] for a in range(4)]
            rows = pl.ds(128 * j, 128)
            o[g, rows, 0:128] = pair_heads(heads[0], heads[1], False).astype(BF)
            o[g, rows, 128:256] = pair_heads(heads[2], heads[3], False).astype(BF)
            lse[g, pl.ds(j, 1), :] = jnp.broadcast_to(total, (512, 128)).T[0:1, :]
            if j == 1:
                pump([ag_cot])
        ov = o[g]

        @pl.loop(0, 4)
        def _(i):
            p[g, i] = dot(o[g, pl.ds(pl.multiple_of(128 * i, 128), 128), :], out_w).astype(BF)

        if turn_no == 0:
            scatter8_core(w, p, core_r, state)
            pump(fl_mlp)
    rs = scatter8_ring(w, p, core_r, hop, fin, state)
    pump([rs])
    pump([rs])
    pump([ag_cot])
    pump(fl_mlp)
    pump([rs])

    @pl.loop(0, 8)
    def _(i):
        rows = pl.ds(pl.multiple_of(i * 16, 16), 16)
        v = x_ref[rows, :].astype(F32) + p[c, x, rows, :].astype(F32) + core_r[3, rows, :].astype(F32)
        v = v + fin[0, rows, :].astype(F32) + fin[1, rows, :].astype(F32)
        h[rows, :] = v
        n2[rows, :] = (v * lax.rsqrt(jnp.mean(v * v, axis=1, keepdims=True) + EPS)).astype(BF)

    w.drain()
    save_n1.wait()
    own_cot.wait()


def forward_attention(lens, tokens, cos, sin, cot, qkv_s, out_s, gate_s, up_s, down_s, cid):
    sds = jax.ShapeDtypeStruct
    vm, hb = pl.BlockSpec(memory_space=VMEM), pl.BlockSpec(memory_space=ANY)
    outs = [
        (sds((128, 2048), F32), vm), (sds((128, 2048), BF), vm), (sds((2, 4, 128, 2048), BF), hb),
        (sds((2, 4, 128, 2048), BF), hb), (sds((2, 4, 512, 128), BF), vm), (sds((2, 4, 4, 128, 128), BF), vm),
        (sds((2, 512, 256), BF), vm), (sds((2, 4, 512), F32), vm), (sds((4, 2, 4, 4, 16, 384), BF), vm),
        (sds((4, 4, 16, 2048), BF), vm), (sds((4, 2, 4, 4, 16, 768), BF), hb), (sds((4, 2, 4, 4, 16, 768), BF), hb),
        (sds((4, 4, 48, 2048), BF), hb),
    ]
    return pl.pallas_call(
        m1_kernel,
        out_shape=[a for a, _ in outs],
        in_specs=[pl.BlockSpec(memory_space=pltpu.SMEM)] + [vm] * 3 + [hb] * 6,
        out_specs=[b for _, b in outs],
        scratch_shapes=[
            VMEM((2, 4, 128, 2048), BF), VMEM((2, 4, 128, 2048), BF), VMEM((4, 128, 2048), BF),
            VMEM((2, 64, 2048), BF), VMEM((2, 128, 2048), BF),
            pltpu.SemaphoreType.DMA((140,)), pltpu.SemaphoreType.DMA((140,)), pltpu.SemaphoreType.DMA((7,)),
        ],
        compiler_params=comm_params(cid, 60),
        name="forward_attention",
    )(lens, tokens, cos, sin, cot, qkv_s, out_s, gate_s, up_s, down_s)


def m2_kernel(n2, h, cot, cg, wgate, wup, wdown,
              dh, da, s2, g_gate, g_up, g_down,
              n2v, cv, wg, wu, wd, dact, a_all, dg_all, du_all, p3, p2, core3, core2, hop, fin, st_w, st_d,
              ssem, rsem, lsem):
    c, x = lax.axis_index("core"), lax.axis_index("x")
    entry([{"x": lax.rem(x + 1, 4)}, {"x": lax.rem(x + 3, 4)}, {"core": 1 - c}])
    w = Mail(ssem, rsem)
    ag = gather8(w, n2, n2v)
    pump([ag])
    loads = [pltpu.make_async_copy(a, b, lsem.at[i]) for i, (a, b) in enumerate(
        ((n2, n2v.at[c, x]), (cg, cv), (wdown, wd), (wgate, wg), (wup, wu)))]
    for cp in loads:
        cp.start()
    loads[1].wait()
    loads[2].wait()
    down = wd[...].reshape(768, 2048)

    @pl.loop(0, 2)
    def _(g):
        for t in range(2):
            dact[g, pl.ds(256 * t, 256), :] = dott(cv[g, 2 * t: 2 * t + 2].reshape(256, 2048), down)

    pump([ag])
    loads[0].wait()
    pump([ag])
    loads[3].wait()
    loads[4].wait()
    gate, up = wg[...].reshape(2048, 768), wu[...].reshape(2048, 768)
    pump([ag])

    def half(g):
        @pl.loop(0, 2)
        def _(t):
            rows = pl.ds(pl.multiple_of(256 * t, 256), 256)
            xv = n2v[g, pl.ds(2 * t, 2)].reshape(256, 2048)
            gp, u = dot(xv, gate), dot(xv, up)
            sig = jax.nn.sigmoid(gp)
            act = gp * sig
            d = dact[g, rows, :]
            a_all[g, rows, :] = (act * u).astype(BF)
            dg_all[g, rows, :] = (d * u * sig * (1.0 + gp * (1.0 - sig))).astype(BF)
            du_all[g, rows, :] = (d * act).astype(BF)

        @pl.loop(0, 8)
        def _(i):
            part = dott(dg_all[g], wg[i // 2, i % 2].reshape(256, 768))
            part += dott(du_all[g], wu[i // 2, i % 2].reshape(256, 768))
            p3[g, :, :, pl.ds(pl.multiple_of(256 * i, 256), 256)] = part.astype(BF).reshape(4, 128, 256)

    g0, g1 = 1 - c, c
    st3, st2 = {}, {}
    half(g0)
    scatter8_core(w, p3, core3, st3)
    half(g1)
    rs3 = scatter8_ring(w, p3, core3, hop, fin, st3)
    pump([rs3])

    def out_part(g):
        @pl.loop(0, 8)
        def _(i):
            cols = pl.ds(pl.multiple_of(256 * i, 256), 256)
            p2[g, :, :, cols] = dot(a_all[g], wd[:, :, :, cols].reshape(768, 256)).astype(BF).reshape(4, 128, 256)

    out_part(g0)
    scatter8_core(w, p2, core2, st2)
    out_part(g1)
    pump([rs3])

    dg, du, av = dg_all[...].reshape(1024, 768), du_all[...].reshape(1024, 768), a_all[...].reshape(1024, 768)

    def stage(i, k):
        return pltpu.make_async_copy(st_w.at[i % 2, k], (g_gate, g_up)[k].at[i // 2, i % 2], lsem.at[5 + 2 * (i % 2) + k])

    for i in range(8):
        t = n2v[:, :, :, 256 * i: 256 * i + 256].reshape(1024, 256).T
        if i >= 2:
            stage(i - 2, 0).wait()
            stage(i - 2, 1).wait()
        st_w[i % 2, 0] = dot(t, dg).astype(BF).reshape(4, 4, 16, 768)
        st_w[i % 2, 1] = dot(t, du).astype(BF).reshape(4, 4, 16, 768)
        stage(i, 0).start()
        stage(i, 1).start()

    cc, xx, right, left, opp, to_r, to_l, to_c = cx_ring()
    for i, b in enumerate((opp, right, left, x)):
        w.got(core2.at[i], st2["k"][i], to_c)
        add_to(p2.at[c, b], core2.at[i], 0, 128)
    save = pltpu.make_async_copy(p2.at[c], s2, lsem.at[9])
    save.start()
    ct = cv[...].reshape(1024, 2048)

    def keep(i):
        return pltpu.make_async_copy(st_d.at[i], g_down.at[pl.ds(i, 1)], lsem.at[10 + i])

    for i in range(4):
        t = av[:, 192 * i: 192 * i + 192].T
        st_d[i] = dot(t, ct).astype(BF).reshape(1, 4, 48, 2048)
        keep(i).start()
    pump([rs3])

    @pl.loop(0, 8)
    def _(i):
        rows = pl.ds(pl.multiple_of(i * 16, 16), 16)
        e = p3[c, x, rows, :].astype(F32) + core3[3, rows, :].astype(F32)
        e = e + fin[0, rows, :].astype(F32) + fin[1, rows, :].astype(F32)
        v = h[rows, :]
        r = lax.rsqrt(jnp.mean(v * v, axis=1, keepdims=True) + EPS)
        out = cot[rows, :].astype(F32) + r * e - v * (r * r * r * jnp.mean(e * v, axis=1, keepdims=True))
        dh[rows, :] = out
        da[rows, :] = out.astype(BF)

    w.drain()
    save.wait()
    for i in (6, 7):
        stage(i, 0).wait()
        stage(i, 1).wait()
    for i in range(4):
        keep(i).wait()


def feed_forward(n2, h, cot, cg, wgate, wup, wdown, cid):
    sds = jax.ShapeDtypeStruct
    vm, hb = pl.BlockSpec(memory_space=VMEM), pl.BlockSpec(memory_space=ANY)
    col = (4, 2, 4, 4, 16, 768)
    outs = [(sds((128, 2048), F32), vm), (sds((128, 2048), BF), vm), (sds((4, 128, 2048), BF), hb),
            (sds(col, BF), hb), (sds(col, BF), hb), (sds((4, 4, 48, 2048), BF), hb)]
    return pl.pallas_call(
        m2_kernel,
        out_shape=[a for a, _ in outs],
        in_specs=[hb, vm, vm, hb, hb, hb, hb],
        out_specs=[b for _, b in outs],
        scratch_shapes=[
            VMEM((2, 4, 128, 2048), BF), VMEM((2, 4, 128, 2048), BF), VMEM(col, BF), VMEM(col, BF),
            VMEM((4, 4, 48, 2048), BF), VMEM((2, 512, 768), F32), VMEM((2, 512, 768), BF), VMEM((2, 512, 768), BF),
            VMEM((2, 512, 768), BF), VMEM((2, 4, 128, 2048), BF), VMEM((2, 4, 128, 2048), BF),
            VMEM((4, 128, 2048), BF), VMEM((4, 128, 2048), BF), VMEM((2, 64, 2048), BF), VMEM((2, 128, 2048), BF),
            VMEM((2, 2, 4, 4, 16, 768), BF), VMEM((4, 1, 4, 48, 2048), BF),
            pltpu.SemaphoreType.DMA((30,)), pltpu.SemaphoreType.DMA((30,)), pltpu.SemaphoreType.DMA((14,)),
        ],
        compiler_params=comm_params(cid, 63),
        name="feed_forward",
    )(n2, h, cot, cg, wgate, wup, wdown)


def ring_tail(w, s, hop, fin):
    c, x, right, left, opp, to_r, to_l, to_c = cx_ring()
    half = s.shape[1] // 2
    lo, hi = pl.ds(0, half), pl.ds(half, half)
    k = [w.new() for _ in range(6)]
    w.put(s.at[opp, lo], hop.at[0], k[0], to_r)
    w.put(s.at[opp, hi], hop.at[1], k[1], to_l)
    w.put(s.at[right, hi], fin.at[0, hi], k[2], to_r)
    w.put(s.at[left, lo], fin.at[1, lo], k[3], to_l)
    yield
    w.got(hop.at[0], k[0], to_l)
    add_to(s.at[right], hop.at[0], 0, half)
    w.put(s.at[right, lo], fin.at[0, lo], k[4], to_r)
    w.got(hop.at[1], k[1], to_r)
    add_to(s.at[left], hop.at[1], half, half)
    w.put(s.at[left, hi], fin.at[1, hi], k[5], to_l)
    yield
    w.got(fin.at[0, hi], k[2], to_l)
    w.got(fin.at[1, lo], k[3], to_r)
    w.got(fin.at[0, lo], k[4], to_l)
    w.got(fin.at[1, hi], k[5], to_r)


def others(w, q, axis, piece, recv):
    ks = {}
    for k in (1, 3, 2):
        to = lax.rem(q + k, 4)
        ks[k] = w.new()
        w.put(piece(to), recv.at[k - 1], ks[k], {axis: to})
    return [(recv.at[k - 1], ks[k], {axis: lax.rem(q + 4 - k, 4)}) for k in (1, 3, 2)]


def sum_four(dst, own, recv, lead):
    total = math.prod(lead)

    @pl.loop(0, total)
    def _(i):
        at = (i,) if len(lead) == 1 else (i // lead[1], lax.rem(i, lead[1]))
        acc = own[at].astype(F32)
        for k in range(3):
            acc += recv[(k,) + at].astype(F32)
        dst[at] = acc.astype(dst.dtype)


def col_job(w, src, r1, t, r2, s, e, z, y, lsem):
    if e == 0:
        own, piece1, ax1, q1 = src.at[:, 0, :, y], lambda p: src.at[:, 0, :, p], "y", y
        piece2, ax2, q2 = lambda p: t.at[p], "z", z
    else:
        own, piece1, ax1, q1 = src.at[z, 1], lambda p: src.at[p, 1], "z", z
        piece2, ax2, q2 = lambda p: t.at[:, p], "y", y
    first = pltpu.make_async_copy(own, t, lsem)
    first.start()
    waits = others(w, q1, ax1, piece1, r1)
    yield
    first.wait()
    for a in waits:
        w.got(*a)
    sum_four(t, t, r1, (4, 4))
    waits = others(w, q2, ax2, piece2, r2)
    yield
    for a in waits:
        w.got(*a)
    sum_four(s.at[e], piece2(q2), r2, (4,))


def row_job(w, src, r1, t, r2, s, e, z, y, lsem):
    n = src.shape[-1] // 2
    rows = src.shape[2]
    cols = pl.ds(e * n, n)
    if e == 0:
        own, piece1, ax1, q1 = src.at[:, y, :, cols], lambda p: src.at[:, p, :, cols], "y", y
        ax2, q2 = "z", z
    else:
        own, piece1, ax1, q1 = src.at[z, :, :, cols], lambda p: src.at[p, :, :, cols], "z", z
        ax2, q2 = "y", y
    first = pltpu.make_async_copy(own, t, lsem)
    first.start()
    waits = others(w, q1, ax1, piece1, r1)
    yield
    first.wait()
    for a in waits:
        w.got(*a)
    sum_four(t, t, r1, (4,))
    waits = others(w, q2, ax2, lambda p: t.at[p], r2)
    yield
    for a in waits:
        w.got(*a)

    @pl.loop(0, rows // 16)
    def _(i):
        at = pl.ds(pl.multiple_of(i * 16, 16), 16)
        acc = t[q2, at].astype(F32)
        for k in range(3):
            acc += r2[k, at].astype(F32)
        s[at, cols] = acc.astype(BF)


def hand_out(w, s, f, c, x):
    r = 2 * x + c
    ks = [w.new() for _ in range(7)]
    for k, (rr, to) in zip(ks, tp_peers(c, x)):
        w.put(s.at[lax.rem(rr, 2), rr // 2], f.at[r], k, to)
    f[r] = s[c, x]
    yield
    for i, k in enumerate(ks):
        rr = lax.rem(r + 7 - i, 8)
        w.got(f.at[rr], k, {"x": rr // 2, "core": lax.rem(rr, 2)})


def m3_kernel(lens, da, dh, x_ref, h, cos, sin, n1g, wqkv, wout, qp, kv, o, lse, s2, g_gate, g_up, g_down,
              out, gt, f_gate, f_up, f_qkv, f_down, f_out,
              dav, n1v, s2v, do4, delta, acc, kvt, dqt, dkv_s, dkv_r, dqkv, p4, core_r, hop, fin, hop2, fin2,
              d_qkv, d_out,
              ra0, ra1, rb0, rb1, rc0, rc1, rd0, rd1, re0, re1,
              ta0, ta1, tb0, tb1, tc0, tc1, td0, td1, te0, te1,
              qa0, qa1, qb0, qb1, qc0, qc1, qd0, qd1, qe0, qe1,
              s_gate, s_up, s_qkv, s_down, s_out, ssem, rsem, lsem):
    z, c, x, y = (lax.axis_index(a) for a in ALL)
    peers = [to for _, to in tp_peers(c, x)]
    for axis, q in (("y", y), ("z", z)):
        peers += [{axis: lax.rem(q + k, 4)} for k in (1, 2, 3)]
    entry(peers, (z != x, {"z": x, "x": z}))
    w = Mail(ssem, rsem)
    ag = gather8(w, da, dav)
    pump([ag])
    loads = [pltpu.make_async_copy(a, b, lsem.at[i]) for i, (a, b) in enumerate(
        ((da, dav.at[c, x]), (s2, s2v), (n1g, n1v)))]
    for cp in loads:
        cp.start()
    jobs = [
        col_job(w, g_gate, ra0, ta0, qa0, s_gate, 0, z, y, lsem.at[3]),
        col_job(w, g_gate, ra1, ta1, qa1, s_gate, 1, z, y, lsem.at[4]),
        col_job(w, g_up, rb0, tb0, qb0, s_up, 0, z, y, lsem.at[5]),
        col_job(w, g_up, rb1, tb1, qb1, s_up, 1, z, y, lsem.at[6]),
        row_job(w, g_down, rc0, tc0, qc0, s_down, 0, z, y, lsem.at[7]),
        row_job(w, g_down, rc1, tc1, qc1, s_down, 1, z, y, lsem.at[8]),
    ]
    pump(jobs)
    pump([ag])
    loads[0].wait()
    pump([ag])
    loads[1].wait()
    tail2 = ring_tail(w, s2v, hop2, fin2)
    pump([tail2])
    pump([ag])

    ow = wout[...].reshape(256, 2048)
    for g in range(2):
        dv = dott(dav[g].reshape(512, 2048), ow).astype(BF).astype(F32)
        ov = o[g].astype(F32)
        for t in range(2):
            v = dv[:, 128 * t: 128 * t + 128]
            pr = v * ov[:, 128 * t: 128 * t + 128]
            low = lanes(v.shape) < 64
            for b, head in enumerate((pltpu.roll(v, 64, 1), v)):
                rows = pl.ds(128 * (2 * t + b), 128)
                do4[g, :, rows, :] = jnp.where(low, 0.0, head).astype(BF).reshape(4, 128, 128)
                total = jnp.sum(jnp.where(low == (b == 0), pr, 0.0), axis=1, keepdims=True)
                total = jnp.broadcast_to(total, (512, 128)).T
                for j in range(4):
                    delta[g, pl.ds(j, 1), rows] = total[0:1, 128 * j: 128 * j + 128]

    ot = o[...].reshape(1024, 256).T

    @pl.loop(0, 8)
    def _(i):
        cols = pl.ds(pl.multiple_of(256 * i, 256), 256)
        d_out[:, :, :, cols] = dot(ot, dav[:, :, :, cols].reshape(1024, 256)).astype(BF).reshape(4, 4, 16, 256)

    jobs_out = [
        row_job(w, d_out, rd0, td0, qd0, s_out, 0, z, y, lsem.at[9]),
        row_job(w, d_out, rd1, td1, qd1, s_out, 1, z, y, lsem.at[10]),
    ]
    pump(jobs_out)

    g0, g1 = 1 - c, c
    waits = {}
    for no, g in enumerate((g0, g1)):
        kvt[...] = kv[g].reshape(2048, 128).T
        acc[...] = jnp.zeros_like(acc)
        for j in range(4):
            qj, doj = qp[g, j], do4[g, j]
            lse_row, delta_row = lse[g, pl.ds(j, 1), :], delta[g, pl.ds(j, 1), :]
            col = lanes((1, 512))
            place = (4 * j + y) * 128 + lax.rem(col, 128)
            start = jnp.where(place >= lens[g, 1], lens[g, 1], jnp.where(place >= lens[g, 0], lens[g, 0], 0))
            dqt[...] = jnp.zeros_like(dqt)

            @pl.loop(0, j + 1)
            def _(b):
                keys = kv[g, b].reshape(512, 128)
                at = 512 * b + lax.broadcasted_iota(jnp.int32, (512, 512), 0)
                ok = (at >= start) & (at <= place)
                pt = jnp.where(ok, jnp.exp(dott(keys, qj) - lse_row), 0.0)
                ds = (pt * (dott(keys, doj) - delta_row)).astype(BF)
                acc[b] += dot(ds, qj) + dot(pt.astype(BF), doj)
                dqt[...] += dot(kvt[:, pl.ds(pl.multiple_of(512 * b, 512), 512)], ds)

            dq = dqt[...].T
            rows = pl.ds(128 * j, 128)
            cs, sn = cos[g, rows, :], sin[g, rows, :]
            for t in range(2):
                v = pair_heads(dq[256 * t: 256 * t + 128], dq[256 * t + 128: 256 * t + 256], True) * (HD ** -0.5)
                dqkv[g, rows, 128 * t: 128 * t + 128] = (v * cs - swap_halves(v) * sn).astype(BF)
            if j == 1:
                if no == 0:
                    pump(jobs[:2])
                    pump([tail2])
                    pump(jobs[2:])
                else:
                    pump(jobs + jobs_out)
                    ends = [hand_out(w, s_gate, f_gate, c, x), hand_out(w, s_up, f_up, c, x),
                            transpose_zx(w, s_down, lambda zz: f_down, z, x, lsem.at[11])]
                    pump(ends)
        dkv_s[no] = acc[...].astype(BF).reshape(4, 4, 128, 128)
        waits[no] = others(w, y, "y", lambda p, no=no: dkv_s.at[no, :, p], dkv_r.at[no])
        if no == 0:
            pump(jobs_out)
    pump([tail2])

    @pl.loop(0, 8)
    def _(i):
        rows = pl.ds(pl.multiple_of(i * 16, 16), 16)
        v = h[rows, :] + s2v[x, rows, :].astype(F32) + fin2[0, rows, :].astype(F32) + fin2[1, rows, :].astype(F32)
        out[rows, :] = v.astype(BF)

    pump(jobs_out)
    tr_out = transpose_zx(w, s_out, lambda zz: f_out, z, x, lsem.at[12])
    pump([tr_out])

    state = {}
    for no, g in enumerate((g0, g1)):
        for a in waits[no]:
            w.got(*a)
        for j in range(4):
            rows = pl.ds(128 * j, 128)
            v = dkv_s[no, j, y].astype(F32)
            for k in range(3):
                v += dkv_r[no, k, j].astype(F32)
            turned = v * cos[g, rows, :] - swap_halves(v) * sin[g, rows, :]
            dqkv[g, rows, 256:384] = jnp.where(lanes(v.shape) < 64, turned, v).astype(BF)

        @pl.loop(0, 8)
        def _(i):
            wt = wqkv[i // 2, i % 2].reshape(256, 384)
            p4[g, :, :, pl.ds(pl.multiple_of(256 * i, 256), 256)] = dott(dqkv[g], wt).astype(BF).reshape(4, 128, 256)

        if no == 0:
            scatter8_core(w, p4, core_r, state)
    rs = scatter8_ring(w, p4, core_r, hop, fin, state)
    pump([rs])
    loads[2].wait()
    dv = dqkv[...].reshape(1024, 384)

    @pl.loop(0, 8)
    def _(i):
        cols = pl.ds(pl.multiple_of(256 * i, 256), 256)
        d_qkv[i // 2, i % 2] = dot(n1v[:, :, :, cols].reshape(1024, 256).T, dv).astype(BF).reshape(4, 4, 16, 384)

    jobs_qkv = [
        col_job(w, d_qkv, re0, te0, qe0, s_qkv, 0, z, y, lsem.at[13]),
        col_job(w, d_qkv, re1, te1, qe1, s_qkv, 1, z, y, lsem.at[14]),
    ]
    pump(jobs_qkv)
    pump([rs])
    pump(jobs_qkv)
    pump(jobs_qkv)
    end_qkv = hand_out(w, s_qkv, f_qkv, c, x)
    pump([end_qkv])
    pump([rs])

    @pl.loop(0, 8)
    def _(i):
        rows = pl.ds(pl.multiple_of(i * 16, 16), 16)
        e = p4[c, x, rows, :].astype(F32) + core_r[3, rows, :].astype(F32)
        e = e + fin[0, rows, :].astype(F32) + fin[1, rows, :].astype(F32)
        v = x_ref[rows, :].astype(F32)
        r = lax.rsqrt(jnp.mean(v * v, axis=1, keepdims=True) + EPS)
        gt[rows, :] = dh[rows, :] + r * e - v * (r * r * r * jnp.mean(e * v, axis=1, keepdims=True))

    pump(ends)
    pump([tr_out, end_qkv])
    w.drain()


def backward_attention(lens, da, dh, x, h, cos, sin, n1g, wqkv, wout, qp, kv, o, lse, s2, g_gate, g_up, g_down, cid):
    sds = jax.ShapeDtypeStruct
    vm, hb = pl.BlockSpec(memory_space=VMEM), pl.BlockSpec(memory_space=ANY)
    outs = [sds((128, 2048), BF), sds((128, 2048), F32), sds((8, 16, 768), BF), sds((8, 16, 768), BF),
            sds((8, 16, 384), BF), sds((48, 2048), BF), sds((16, 2048), BF)]
    b = lambda *s: VMEM(s, BF)
    r1 = [b(3, 4, 4, 16, 768)] * 4 + [b(3, 4, 48, 1024)] * 2 + [b(3, 4, 16, 1024)] * 2 + [b(3, 4, 4, 16, 384)] * 2
    t1 = [b(4, 4, 16, 768)] * 4 + [b(4, 48, 1024)] * 2 + [b(4, 16, 1024)] * 2 + [b(4, 4, 16, 384)] * 2
    r2 = [b(3, 4, 16, 768)] * 4 + [b(3, 48, 1024)] * 2 + [b(3, 16, 1024)] * 2 + [b(3, 4, 16, 384)] * 2
    return pl.pallas_call(
        m3_kernel,
        out_shape=outs,
        in_specs=[pl.BlockSpec(memory_space=pltpu.SMEM), hb] + [vm] * 5 + [hb] + [vm] * 6 + [hb] * 4,
        out_specs=[vm] * 7,
        scratch_shapes=[
            b(2, 4, 128, 2048), b(2, 4, 128, 2048), b(4, 128, 2048), b(2, 4, 512, 128), VMEM((2, 4, 512), F32),
            VMEM((4, 512, 128), F32), b(128, 2048), VMEM((128, 512), F32), b(2, 4, 4, 128, 128),
            b(2, 3, 4, 128, 128), b(2, 512, 384), b(2, 4, 128, 2048), b(4, 128, 2048), b(2, 64, 2048),
            b(2, 128, 2048), b(2, 64, 2048), b(2, 128, 2048), b(4, 2, 4, 4, 16, 384), b(4, 4, 16, 2048),
        ] + r1 + t1 + r2 + [
            b(2, 4, 16, 768), b(2, 4, 16, 768), b(2, 4, 16, 384), b(48, 2048), b(16, 2048),
            pltpu.SemaphoreType.DMA((130,)), pltpu.SemaphoreType.DMA((130,)), pltpu.SemaphoreType.DMA((15,)),
        ],
        compiler_params=comm_params(cid, 63),
        name="backward_attention",
    )(lens, da, dh, x, h, cos, sin, n1g, wqkv, wout, qp, kv, o, lse, s2, g_gate, g_up, g_down)


def local(tokens, lengths, attn_gain, w_query, w_key, w_value, w_out, mlp_gain, w_gate, w_up, w_down, cotangent):
    y = lax.axis_index("y")
    gain1 = attn_gain.astype(F32)[:, None]
    gain2 = mlp_gain.astype(F32)[:, None]
    fold = lambda w, g: (w.astype(F32) * g).astype(BF)
    ranks_first = lambda w: w.transpose(1, 0, 2)
    pad_ff = lambda w: jnp.pad(w.reshape(16, 8, 16, 44), ((0, 0), (0, 0), (0, 0), (0, 4))).reshape(16, 8, 768)
    twice = lambda w: jnp.repeat(w.reshape(16, 4, HD), 2, axis=1)
    qkv_s = ranks_first(jnp.concatenate(
        [fold(w_query, gain1).reshape(16, 8, 256), twice(fold(w_key, gain1)), twice(fold(w_value, gain1))], axis=2))
    gate_s, up_s = ranks_first(pad_ff(fold(w_gate, gain2))), ranks_first(pad_ff(fold(w_up, gain2)))
    down_s = jnp.pad(w_down, ((0, 4), (0, 0)))

    both = lax.all_gather(lengths, "core", axis=0, tiled=True)
    place = ((4 * jnp.arange(4)[:, None] + y) * 128 + jnp.arange(128)[None, :]).reshape(1, 512).astype(jnp.int32)
    c1, c2 = both[:, 0:1], both[:, 0:1] + both[:, 1:2]
    lens = jnp.concatenate([c1, c2], axis=1)
    start = jnp.where(place >= c2, c2, jnp.where(place >= c1, c1, 0))
    lane = jnp.arange(128) % 32
    frequency = jnp.exp(lane.astype(F32) * (-2.0 * math.log(THETA) / HD))
    sign = jnp.where(jnp.arange(128) % 64 < 32, -1.0, 1.0)
    angle = (place - start)[:, :, None].astype(F32) * frequency
    cos, sin = jnp.cos(angle), jnp.sin(angle) * sign

    h, n2, n1g, cg, qp, kv, o, lse, wqkv, wout, wgate, wup, wdown = forward_attention(
        lens, tokens, cos, sin, cotangent, qkv_s, w_out, gate_s, up_s, down_s, 1)
    dh, da, s2, g_gate, g_up, g_down = feed_forward(n2, h, cotangent, cg, wgate, wup, wdown, 2)
    output, grad_tokens, gate_s, up_s, qkv_s, down_s, out_s = backward_attention(
        lens, da, dh, tokens, h, cos, sin, n1g, wqkv, wout, qp, kv, o, lse, s2, g_gate, g_up, g_down, 3)

    wide = lambda v: v.astype(F32).transpose(1, 0, 2).reshape(16, -1)
    unpad = lambda v: v.reshape(16, 128, 48)[:, :, :44].reshape(16, 5632)
    g_gate, g_up = unpad(wide(gate_s)), unpad(wide(up_s))
    pair = lambda v: v.astype(F32).reshape(4, 2, 16, HD).sum(axis=1).transpose(1, 0, 2).reshape(16, -1)
    g_query, g_key, g_value = wide(qkv_s[..., :256]), pair(qkv_s[..., 256:320]), pair(qkv_s[..., 320:])
    rowdot = lambda w, gr: jnp.sum(w.astype(F32) * gr, axis=1)
    grad_attn_gain = rowdot(w_query, g_query) + rowdot(w_key, g_key) + rowdot(w_value, g_value)
    grad_mlp_gain = rowdot(w_gate, g_gate) + rowdot(w_up, g_up)
    return (output, grad_tokens, grad_attn_gain, gain1 * g_query, gain1 * g_key, gain1 * g_value,
            out_s.astype(F32), grad_mlp_gain, gain2 * g_gate, gain2 * g_up, down_s[:44].astype(F32))


def solution(mesh):
    fine = Mesh(mesh.devices.reshape(4, 2, 4, 4), ALL)
    rows, flat = P(ALL, None), P(ALL)
    in_specs = (rows, P(("z", "core"), None), flat, rows, rows, rows, rows, flat, rows, rows, rows, rows)
    out_specs = (rows, rows, flat, rows, rows, rows, rows, flat, rows, rows, rows)
    return jax.shard_map(local, mesh=fine, in_specs=in_specs, out_specs=out_specs, check_vma=False)
```

time: 4920 us -> 374 us (0.08)
  waiting for transfers between devices: 3610 us -> 0 us
  blocking collectives: 750 us -> 3.01 us
  Pallas kernels: 0 us -> 334 us
  matrix products: 261 us -> 0 us
  local copies, waits for them, and re-layouts: 101 us -> 14.9 us
  starting transfers between devices: 76.4 us -> 0 us
    reduce_scatter x6 -> x0, waiting for transfers between devices: 3230 us -> none  [the longest x1 743 us: local(): lax.psum_scatter(grad_wgate, ('batch', 'seq'), scatter_dimension=0, tiled...]
    unnamed x3 -> x0, blocking collectives: 712 us -> none
    pallas_call x0 -> x3, Pallas kernels: none -> 334 us  [the longest x1 137 us: forward_attention(): pl.pallas_call(m1_kernel, out_shape=[a for a, _ in outs], in_specs=[pl.Bl...]
    all_gather x7 -> x0, waiting for transfers between devices: 321 us -> none  [the longest x1 80.2 us: local(): lax.all_gather(w_gate, ('batch', 'seq'), axis=0, tiled=True)]
    dot_general x49 -> x0, matrix products: 261 us -> none  [the longest x7 77.6 us: left_dot(): lax.dot_general(left_arg, right_arg, (((0,), (0,)), ((), ())), preferred_...]
    unnamed x74 -> x16, local copies, waits for them, and re-layouts: 71.6 us -> 2.89 us
    unnamed x11 -> x0, starting transfers between devices: 50.6 us -> none
  transfers between devices with their start and end apart: 29 -> 0, of which waited for: 20 -> 0; matrix products, arithmetic and copies ran while one was open for 17% -> 0% of each run, Pallas kernels for 0% -> 0%
where the time goes in v1:
time: 374 us; the launch traced here: 370 us
  Pallas kernels  334 us (89%)
  other arithmetic  16.9 us (5%)
  local copies, waits for them, and re-layouts  14.9 us (4%)
    pallas_call x1, Pallas kernels, forward_attention(): pl.pallas_call(m1_kernel, out_shape=[a for a, _ in outs], in_specs=[pl.Bl...  137 us
    pallas_call x1, Pallas kernels, backward_attention(): pl.pallas_call(m3_kernel, out_shape=outs, in_specs=[pl.BlockSpec(memory_s...  131 us
    pallas_call x1, Pallas kernels, feed_forward(): pl.pallas_call(m2_kernel, out_shape=[a for a, _ in outs], in_specs=[hb, v...  66.3 us

profile of v1, /device:TPU:1, one launch (start us, length us, event | category | flops | bytes accessed | tf_op | source)
XLA Modules:
  0.0 370.4 jit_solution(18098756742660277221)
XLA Ops:
  0.7 0.7 convert_element_type.75
  1.3 0.7 convert_element_type.82
  2.0 3.0 all-gather
  5.0 0.1 add_bitcast_fusion
  5.1 0.2 fusion.16
  5.2 0.6 pad_add_fusion.lens
  5.9 0.1 fusion.12
  6.0 0.8 fusion.7
  6.8 0.1 reshape.242
  6.9 0.1 reshape.244
  7.0 0.9 fusion.5
  7.9 0.7 maximum_bitcast_fusion.qkv_s
  8.6 1.6 pad.13.down_s
  10.3 1.1 fusion.3
  11.4 1.5 reshape.248
  12.9 0.1 pad.12
  13.0 1.1 reshape.249
  14.2 1.5 reshape.246
  15.7 0.1 pad.11
  15.9 1.2 reshape.247
  17.0 3.0 fusion
  20.0 136.7 %forward_attention.1 = (f32[128,2048]{1,0:T(8,128)}, bf16[128,2048]{1,0:T(8,128)(2,1)}, bf16[2,4,128,2048]{3,2,1,0:T(8,128)(2,1)}, bf16[2,4,128,2048]{3,2,1,0:T(...) custom-call(s32[2,2]{1,0:T(2,128)} %pad_add_fusion.lens, ...), custom_call_target="tpu_custom_call" | custom-call | tf_op jit(solution)/shard_map/forward_attention/pallas_call | solution.py:457
  156.8 66.3 %feed_forward.1 = (f32[128,2048]{1,0:T(8,128)}, bf16[128,2048]{1,0:T(8,128)(2,1)}, bf16[4,128,2048]{2,1,0:T(8,128)(2,1)}, bf16[4,2,4,4,16,768]{5,4,3,2,1,0:T(8,1...) custom-call(bf16[128,2048]{1,0:T(8,128)(2,1)} %get-tuple-element.37.n2, ...), custom_call_target="tpu_custom_call" | custom-call | tf_op jit(solution)/shard_map/feed_forward/pallas_call | solution.py:598
  223.1 0.0 copy-start.5
  223.1 0.0 copy-start.6
  223.1 0.0 copy-start.3
  223.1 131.4 %backward_attention.1 = (bf16[128,2048]{1,0:T(8,128)(2,1)}, f32[128,2048]{1,0:T(8,128)}, bf16[8,16,768]{2,1,0:T(8,128)(2,1)}, bf16[8,16,768]{2,1,0:T(8,128)(2,1)...) custom-call(s32[2,2]{1,0:T(2,128)} %pad_add_fusion.lens, ...), custom_call_target="tpu_custom_call" | custom-call | tf_op jit(solution)/shard_map/backward_attention/pallas_call | solution.py:911
  354.6 0.0 copy-start.4
  354.6 0.9 convert_reduce_fusion.1
  355.5 0.1 reshape.254
  355.6 0.1 reshape.257
  355.7 0.0 copy-done.5
  355.7 0.0 copy-done.6
  355.7 0.8 broadcast_multiply_fusion.3
  356.5 0.9 convert_bitcast_fusion
  357.4 0.0 copy-done.3
  357.4 0.8 broadcast_multiply_fusion.2
  358.2 0.5 add_add_fusion
  358.8 1.5 convert_element_type.86
  360.3 1.0 copy.51
  361.3 1.0 copy.52
  362.2 0.6 reshape_reshape.9
  362.9 0.6 reshape_reshape.8
  363.5 0.0 copy-done.4
  363.5 0.0 copy-start.1
  363.5 0.0 copy-start.2
  363.6 0.8 slice_convert_fusion.2
  364.3 0.1 slice_convert_fusion.1
  364.4 0.6 reshape.269
  365.0 0.0 copy-start
  365.0 0.1 slice_convert_fusion
  365.1 0.6 reshape.271
  365.7 0.0 copy-done.1
  365.8 0.0 copy-done.2
  365.8 1.1 broadcast_multiply_fusion
  366.8 0.5 add.81
  367.4 1.9 copy.59
  369.2 0.0 copy-done
  369.2 1.0 copy.60
  (12 shorter events, 0.2 us)
Async XLA Ops:
  223.1 132.6 %copy-start.5 = (bf16[16,256]{1,0:T(8,128)(2,1)S(1)}, bf16[16,256]{1,0:T(8,128)(2,1)}, u32[]{:S(2)}) copy-start(bf16[16,256]{1,0:T(8,128)(2,1)} %param.16) | copy-start | bytes 24580
  223.1 132.6 %copy-start.6 = (bf16[16,256]{1,0:T(8,128)(2,1)S(1)}, bf16[16,256]{1,0:T(8,128)(2,1)}, u32[]{:S(2)}) copy-start(bf16[16,256]{1,0:T(8,128)(2,1)} %param.17) | copy-start | bytes 24580
  223.1 134.3 %copy-start.3 = (bf16[16,2048]{1,0:T(8,128)(2,1)S(1)}, bf16[16,2048]{1,0:T(8,128)(2,1)}, u32[]{:S(2)}) copy-start(bf16[16,2048]{1,0:T(8,128)(2,1)} %param.15) | copy-start | bytes 196612
  354.6 9.0 %copy-start.4 = (bf16[48,2048]{1,0:T(8,128)(2,1)S(1)}, bf16[48,2048]{1,0:T(8,128)(2,1)}, u32[]{:S(2)}) copy-start(bf16[48,2048]{1,0:T(8,128)(2,1)} %get-tuple-element.62) | copy-start | bytes 589828
  363.5 2.2 copy-start.1
  363.5 2.2 copy-start.2
  365.0 4.2 %copy-start = (f32[128,2048]{1,0:T(8,128)S(1)}, f32[128,2048]{1,0:T(8,128)}, u32[]{:S(2)}) copy-start(f32[128,2048]{1,0:T(8,128)} %get-tuple-element.103) | copy-start | bytes 3145732

commit v2 on v1

--- a/solution.py
+++ b/solution.py
@@ -46,6 +46,13 @@
             device_id=to, device_id_type=pl.DeviceIdType.MESH)
         cp.start()
         self.sent.append(cp)
+        return cp
+
+    def settle(self, copies):
+        for cp in copies:
+            cp.wait_send()
+        done = {id(cp) for cp in copies}
+        self.sent = [cp for cp in self.sent if id(cp) not in done]
 
     def got(self, dst, k, to):
         pltpu.make_async_remote_copy(
@@ -134,6 +141,30 @@
     return [first(), second()]
 
 
+def straight(w, stages):
+    for s, axis, q in stages:
+        ks = {}
+        for k in (1, 3, 2):
+            ks[k] = w.new()
+            w.put(s(q), s(q), ks[k], {axis: lax.rem(q + k, 4)})
+        yield
+        for k in (1, 3, 2):
+            frm = lax.rem(q + 4 - k, 4)
+            w.got(s(frm), ks[k], {axis: frm})
+
+
+def col_straight(w, W, z, y):
+    return [straight(w, [(lambda p: W.at[z, 0, :, p], "y", y), (lambda p: W.at[p, 0], "z", z)]),
+            straight(w, [(lambda p: W.at[p, 1, :, y], "z", z), (lambda p: W.at[:, 1, :, p], "y", y)])]
+
+
+def row_straight(w, W, z, y):
+    n = W.shape[-1] // 2
+    a, b = pl.ds(0, n), pl.ds(n, n)
+    return [straight(w, [(lambda p: W.at[z, p, :, a], "y", y), (lambda p: W.at[p, :, :, a], "z", z)]),
+            straight(w, [(lambda p: W.at[p, y, :, b], "z", z), (lambda p: W.at[:, p, :, b], "y", y)])]
+
+
 def pump(flows):
     for f in flows:
         next(f, None)
@@ -143,28 +174,33 @@
     c, x, right, left, opp, to_r, to_l, to_c = cx_ring()
     rows = dst.shape[2]
     lo, hi = pl.ds(0, rows // 2), pl.ds(rows // 2, rows // 2)
-    k = [w.new() for _ in range(9)]
-    w.put(src, dst.at[c, x], k[0], to_r)
-    w.put(src, dst.at[c, x], k[1], to_l)
-    w.put(src, dst.at[c, x], k[4], to_c)
-    yield
-    w.got(dst.at[c, left], k[0], to_l)
-    w.put(dst.at[c, left, lo], dst.at[c, left, lo], k[2], to_r)
-    w.put(dst.at[c, left], dst.at[c, left], k[5], to_c)
-    w.got(dst.at[c, right], k[1], to_r)
-    w.put(dst.at[c, right, hi], dst.at[c, right, hi], k[3], to_l)
-    w.put(dst.at[c, right], dst.at[c, right], k[6], to_c)
-    yield
-    w.got(dst.at[c, opp, lo], k[2], to_l)
-    w.put(dst.at[c, opp, lo], dst.at[c, opp, lo], k[7], to_c)
-    w.got(dst.at[c, opp, hi], k[3], to_r)
-    w.put(dst.at[c, opp, hi], dst.at[c, opp, hi], k[8], to_c)
+    k = [w.new() for _ in range(10)]
+    out = []
+    out += [w.put(src.at[lo], dst.at[c, x, lo], k[0], to_r)]
+    out += [w.put(src.at[hi], dst.at[c, x, hi], k[1], to_l)]
+    out += [w.put(src.at[hi], dst.at[c, x, hi], k[2], to_r)]
+    out += [w.put(src.at[lo], dst.at[c, x, lo], k[3], to_l)]
+    out += [w.put(src, dst.at[c, x], k[4], to_c)]
+    yield
+    w.got(dst.at[c, left, lo], k[0], to_l)
+    out += [w.put(dst.at[c, left, lo], dst.at[c, left, lo], k[5], to_r)]
+    w.got(dst.at[c, right, hi], k[1], to_r)
+    out += [w.put(dst.at[c, right, hi], dst.at[c, right, hi], k[6], to_l)]
+    yield
+    w.got(dst.at[c, left, hi], k[2], to_l)
+    out += [w.put(dst.at[c, left], dst.at[c, left], k[7], to_c)]
+    w.got(dst.at[c, right, lo], k[3], to_r)
+    out += [w.put(dst.at[c, right], dst.at[c, right], k[8], to_c)]
+    yield
+    w.got(dst.at[c, opp, lo], k[5], to_l)
+    w.got(dst.at[c, opp, hi], k[6], to_r)
+    out += [w.put(dst.at[c, opp], dst.at[c, opp], k[9], to_c)]
     yield
     w.got(dst.at[1 - c, x], k[4], to_c)
-    w.got(dst.at[1 - c, left], k[5], to_c)
-    w.got(dst.at[1 - c, right], k[6], to_c)
-    w.got(dst.at[1 - c, opp, lo], k[7], to_c)
-    w.got(dst.at[1 - c, opp, hi], k[8], to_c)
+    w.got(dst.at[1 - c, left], k[7], to_c)
+    w.got(dst.at[1 - c, right], k[8], to_c)
+    w.got(dst.at[1 - c, opp], k[9], to_c)
+    w.settle(out)
 
 
 def add_to(dst, other, r0, rows, step=16):
@@ -178,8 +214,8 @@
 def scatter8_core(w, p, core_r, state):
     c, x, right, left, opp, to_r, to_l, to_c = cx_ring()
     state["k"] = [w.new() for _ in range(4)]
-    for i, xx in enumerate((opp, right, left, x)):
-        w.put(p.at[1 - c, xx], core_r.at[i], state["k"][i], to_c)
+    state["out"] = [
+        w.put(p.at[1 - c, xx], core_r.at[i], state["k"][i], to_c) for i, xx in enumerate((opp, right, left, x))]
 
 
 def scatter8_ring(w, p, core_r, hop, fin, state):
@@ -187,31 +223,32 @@
     rows = p.shape[2]
     half = rows // 2
     lo, hi = pl.ds(0, half), pl.ds(half, half)
-    kc = state["k"]
+    kc, out = state["k"], state["out"]
     k = [w.new() for _ in range(6)]
     w.got(core_r.at[0], kc[0], to_c)
     add_to(p.at[c, opp], core_r.at[0], 0, rows)
-    w.put(p.at[c, opp, lo], hop.at[0], k[0], to_r)
-    w.put(p.at[c, opp, hi], hop.at[1], k[1], to_l)
+    out += [w.put(p.at[c, opp, lo], hop.at[0], k[0], to_r)]
+    out += [w.put(p.at[c, opp, hi], hop.at[1], k[1], to_l)]
     w.got(core_r.at[1], kc[1], to_c)
     add_to(p.at[c, right], core_r.at[1], 0, rows)
-    w.put(p.at[c, right, hi], fin.at[0, hi], k[2], to_r)
+    out += [w.put(p.at[c, right, hi], fin.at[0, hi], k[2], to_r)]
     w.got(core_r.at[2], kc[2], to_c)
     add_to(p.at[c, left], core_r.at[2], 0, rows)
-    w.put(p.at[c, left, lo], fin.at[1, lo], k[3], to_l)
+    out += [w.put(p.at[c, left, lo], fin.at[1, lo], k[3], to_l)]
     yield
     w.got(hop.at[0], k[0], to_l)
     add_to(p.at[c, right], hop.at[0], 0, half)
-    w.put(p.at[c, right, lo], fin.at[0, lo], k[4], to_r)
+    out += [w.put(p.at[c, right, lo], fin.at[0, lo], k[4], to_r)]
     w.got(hop.at[1], k[1], to_r)
     add_to(p.at[c, left], hop.at[1], half, half)
-    w.put(p.at[c, left, hi], fin.at[1, hi], k[5], to_l)
+    out += [w.put(p.at[c, left, hi], fin.at[1, hi], k[5], to_l)]
     yield
     w.got(core_r.at[3], kc[3], to_c)
     w.got(fin.at[0, hi], k[2], to_l)
     w.got(fin.at[1, lo], k[3], to_r)
     w.got(fin.at[0, lo], k[4], to_l)
     w.got(fin.at[1, hi], k[5], to_r)
+    w.settle(out)
 
 
 def lanes(shape):
@@ -298,12 +335,12 @@
 
 
 def attend(q, keys, j, y, c1, c2):
-    n = keys.shape[0]
+    m, n = q.shape[0], keys.shape[0]
     s = dott(q, keys)
-    row = lax.broadcasted_iota(jnp.int32, (512, 1), 0)
+    row = lax.broadcasted_iota(jnp.int32, (m, 1), 0)
     place = (4 * j + y) * 128 + lax.rem(row, 128)
     start = jnp.where(place >= c2, c2, jnp.where(place >= c1, c1, 0))
-    at = lax.broadcasted_iota(jnp.int32, (512, n), 1)
+    at = lax.broadcasted_iota(jnp.int32, (m, n), 1)
     s = jnp.where((at >= start) & (at <= place), s, NEG)
     top = jnp.max(s, axis=1, keepdims=True)
     e = jnp.exp(s - top)
@@ -318,15 +355,24 @@
     return jnp.where(low, pltpu.roll(first, 64, 1), second)
 
 
-def m1_kernel(lens, x_ref, cos, sin, cot, qkv_s, out_s, gate_s, up_s, down_s,
-              h, n2, n1_out, cg, qp, kv, o, lse, wqkv, wout, wgate, wup, wdown,
-              n1, p, core_r, hop, fin, ssem, rsem, lsem):
+def forward_kernel(lens, x_ref, cos_in, sin_in, cot, qkv_s, out_s, gate_s, up_s, down_s,
+                   h_out, n1_out, qp_out, kv_out, o_out, lse_out, wqkv_out, wout_out,
+                   dh_out, da_out, s2, g_gate, g_up, g_down, r1_down,
+                   cos, sin, h, qp, kv, o, lse, wqkv, wout, n1, cv, wg, wu, wd, p, core_r, hop, fin,
+                   dact, a_all, dg_all, du_all, core2, d_down, ssem, rsem, lsem, osem):
     z, c, x, y = (lax.axis_index(a) for a in ALL)
     peers = [to for _, to in tp_peers(c, x)]
     for axis, q in (("y", y), ("z", z)):
-        peers += [{axis: lax.rem(q + 1, 4)}, {axis: lax.rem(q + 3, 4)}]
+        peers += [{axis: lax.rem(q + k, 4)} for k in (1, 2, 3)]
     entry(peers, (z != x, {"z": x, "x": z}))
     w = Mail(ssem, rsem)
+    saved = []
+
+    def save(src, dst):
+        cp = pltpu.make_async_copy(src, dst, osem.at[len(saved)])
+        cp.start()
+        saved.append(cp)
+        return cp
 
     sp_qkv = spread(w, qkv_s, wqkv, z, c, x, y, lsem.at[0])
     pump([sp_qkv])
@@ -340,40 +386,34 @@
     ag_n1 = gather8(w, n1.at[c, x], n1)
     pump([ag_n1])
     tr_out = transpose_zx(w, out_s, lambda zz: wout.at[zz, y], z, x, lsem.at[1])
-    sp_gate = spread(w, gate_s, wgate, z, c, x, y, lsem.at[2])
-    sp_up = spread(w, up_s, wup, z, c, x, y, lsem.at[3])
-    tr_down = transpose_zx(w, down_s, lambda zz: wdown.at[zz, y], z, x, lsem.at[4])
-    early = [tr_out, sp_gate, sp_up, tr_down]
-    pump(early)
+    pump([tr_out])
+    tables = [pltpu.make_async_copy(cos_in, cos, lsem.at[5]), pltpu.make_async_copy(sin_in, sin, lsem.at[6])]
+    for cp in tables:
+        cp.start()
     pump([sp_qkv])
-    fl_qkv = col_flows(w, wqkv, z, y)
+    fl_qkv = col_straight(w, wqkv, z, y)
     pump(fl_qkv)
-    pump(early)
-    fl_qkv_out = fl_qkv + row_flows(w, wout, z, y)
-    pump(fl_qkv_out[2:])
-    pump(fl_qkv_out)
-    pump(fl_qkv_out)
     pump([ag_n1])
-    fl_mlp = col_flows(w, wgate, z, y) + col_flows(w, wup, z, y) + row_flows(w, wdown, z, y)
-    pump(fl_mlp)
-    pump(fl_qkv_out)
+    pump(fl_qkv)
+    pump([tr_out])
+    fl_out = row_straight(w, wout, z, y)
+    pump(fl_out)
     pump([ag_n1])
-    pump(fl_qkv_out)
+    pump(fl_out)
     pump([ag_n1])
-    pump(fl_mlp)
-
-    save_n1 = pltpu.make_async_copy(n1, n1_out, lsem.at[5])
-    save_n1.start()
-    own_cot = pltpu.make_async_copy(cot, cg.at[c, x], lsem.at[6])
-    own_cot.start()
-    ag_cot = gather8(w, cot, cg)
-    pump([ag_cot])
-
+    pump(fl_qkv)
+    pump([ag_n1])
+    for cp in tables:
+        cp.wait()
     weights = wqkv[...].reshape(2048, 384)
 
     def project(g, keys_too):
         u = dot(n1[g].reshape(512, 2048), weights)
         cs, sn = cos[g], sin[g]
+        if keys_too:
+            v = u[:, 256:384]
+            turned = jnp.where(lanes(v.shape) < 64, v * cs + swap_halves(v) * sn, v)
+            kv[g, :, y] = turned.astype(BF).reshape(4, 128, 128)
         for t in range(2):
             v = u[:, 128 * t: 128 * t + 128]
             v = (v * cs + swap_halves(v) * sn) * (HD ** -0.5)
@@ -381,54 +421,65 @@
             for b, head in enumerate((v, pltpu.roll(v, 64, 1))):
                 rows = pl.ds(128 * (2 * t + b), 128)
                 qp[g, :, rows, :] = jnp.where(low, head, 0.0).astype(BF).reshape(4, 128, 128)
-        if keys_too:
-            v = u[:, 256:384]
-            turned = jnp.where(lanes(v.shape) < 64, v * cs + swap_halves(v) * sn, v)
-            kv[g, :, y] = turned.astype(BF).reshape(4, 128, 128)
 
     g0, g1 = 1 - c, c
     to_c = {"core": 1 - c}
     project(g0, True)
-    halves = lambda h: slice(None) if h is None else pl.ds(2 * h, 2)
-    fl_kv = [ring(w, lambda pp, hh: kv.at[g0, halves(hh), pp], "y", y)]
+    fl_kv = [straight(w, [(lambda pp: kv.at[g0, :, pp], "y", y)])]
     pump(fl_kv)
+    spreads = [spread(w, gate_s, wg, z, c, x, y, lsem.at[2]), spread(w, up_s, wu, z, c, x, y, lsem.at[3]),
+               transpose_zx(w, down_s, lambda zz: wd.at[zz, y], z, x, lsem.at[4])]
+    pump(spreads)
     project(g1, False)
-    pump(fl_mlp)
-    pump(fl_kv)
+    keep_n1 = save(n1, n1_out)
+    save(wqkv, wqkv_out)
+    keep_cot = save(cot, cv.at[c, x])
+    pump(fl_out)
     pump(fl_kv)
     k_kv = w.new()
     w.put(kv.at[g0], kv.at[g0], k_kv, to_c)
+    pump(spreads)
+    fl_mlp = col_flows(w, wg, z, y) + col_flows(w, wu, z, y) + row_flows(w, wd, z, y)
+    pump(fl_mlp)
+    ag_cot = gather8(w, cot, cv)
+    pump([ag_cot])
 
     state = {}
     out_w = wout[...].reshape(256, 2048)
     for turn_no, g in enumerate((g0, g1)):
         if turn_no == 1:
             w.got(kv.at[g], k_kv, to_c)
+            save(kv, kv_out)
+            save(qp, qp_out)
+            save(wout, wout_out)
         for j in range(4):
             n = 512 * (j + 1)
             keys = kv[g, 0:j + 1].reshape(n, 128)
-            res, total = attend(qp[g, j], keys, j, y, lens[g, 0], lens[g, 1])
-            heads = [res[128 * a: 128 * a + 128] for a in range(4)]
-            rows = pl.ds(128 * j, 128)
-            o[g, rows, 0:128] = pair_heads(heads[0], heads[1], False).astype(BF)
-            o[g, rows, 128:256] = pair_heads(heads[2], heads[3], False).astype(BF)
-            lse[g, pl.ds(j, 1), :] = jnp.broadcast_to(total, (512, 128)).T[0:1, :]
-            if j == 1:
-                pump([ag_cot])
-        ov = o[g]
+            for t in range(2):
+                res, total = attend(qp[g, j, 256 * t: 256 * t + 256], keys, j, y, lens[g, 0], lens[g, 1])
+                both = pair_heads(res[:128], res[128:], False)
+                o[g, pl.ds(128 * j, 128), 128 * t: 128 * t + 128] = both.astype(BF)
+                lse[g, pl.ds(j, 1), 256 * t: 256 * t + 256] = jnp.broadcast_to(total, (256, 128)).T[0:1, :]
+            if turn_no == 0 and j == 2:
+                pump(fl_mlp)
+        pump([ag_cot])
 
         @pl.loop(0, 4)
         def _(i):
             p[g, i] = dot(o[g, pl.ds(pl.multiple_of(128 * i, 128), 128), :], out_w).astype(BF)
 
         if turn_no == 0:
+            keep_n1.wait()
             scatter8_core(w, p, core_r, state)
             pump(fl_mlp)
+            pump([ag_cot])
     rs = scatter8_ring(w, p, core_r, hop, fin, state)
     pump([rs])
+    pump([ag_cot])
+    save(o, o_out)
+    save(lse, lse_out)
     pump([rs])
     pump([ag_cot])
-    pump(fl_mlp)
     pump([rs])
 
     @pl.loop(0, 8)
@@ -437,65 +488,25 @@
         v = x_ref[rows, :].astype(F32) + p[c, x, rows, :].astype(F32) + core_r[3, rows, :].astype(F32)
         v = v + fin[0, rows, :].astype(F32) + fin[1, rows, :].astype(F32)
         h[rows, :] = v
-        n2[rows, :] = (v * lax.rsqrt(jnp.mean(v * v, axis=1, keepdims=True) + EPS)).astype(BF)
-
-    w.drain()
-    save_n1.wait()
-    own_cot.wait()
-
-
-def forward_attention(lens, tokens, cos, sin, cot, qkv_s, out_s, gate_s, up_s, down_s, cid):
-    sds = jax.ShapeDtypeStruct
-    vm, hb = pl.BlockSpec(memory_space=VMEM), pl.BlockSpec(memory_space=ANY)
-    outs = [
-        (sds((128, 2048), F32), vm), (sds((128, 2048), BF), vm), (sds((2, 4, 128, 2048), BF), hb),
-        (sds((2, 4, 128, 2048), BF), hb), (sds((2, 4, 512, 128), BF), vm), (sds((2, 4, 4, 128, 128), BF), vm),
-        (sds((2, 512, 256), BF), vm), (sds((2, 4, 512), F32), vm), (sds((4, 2, 4, 4, 16, 384), BF), vm),
-        (sds((4, 4, 16, 2048), BF), vm), (sds((4, 2, 4, 4, 16, 768), BF), hb), (sds((4, 2, 4, 4, 16, 768), BF), hb),
-        (sds((4, 4, 48, 2048), BF), hb),
-    ]
-    return pl.pallas_call(
-        m1_kernel,
-        out_shape=[a for a, _ in outs],
-        in_specs=[pl.BlockSpec(memory_space=pltpu.SMEM)] + [vm] * 3 + [hb] * 6,
-        out_specs=[b for _, b in outs],
-        scratch_shapes=[
-            VMEM((2, 4, 128, 2048), BF), VMEM((2, 4, 128, 2048), BF), VMEM((4, 128, 2048), BF),
-            VMEM((2, 64, 2048), BF), VMEM((2, 128, 2048), BF),
-            pltpu.SemaphoreType.DMA((140,)), pltpu.SemaphoreType.DMA((140,)), pltpu.SemaphoreType.DMA((7,)),
-        ],
-        compiler_params=comm_params(cid, 60),
-        name="forward_attention",
-    )(lens, tokens, cos, sin, cot, qkv_s, out_s, gate_s, up_s, down_s)
-
-
-def m2_kernel(n2, h, cot, cg, wgate, wup, wdown,
-              dh, da, s2, g_gate, g_up, g_down,
-              n2v, cv, wg, wu, wd, dact, a_all, dg_all, du_all, p3, p2, core3, core2, hop, fin, st_w, st_d,
-              ssem, rsem, lsem):
-    c, x = lax.axis_index("core"), lax.axis_index("x")
-    entry([{"x": lax.rem(x + 1, 4)}, {"x": lax.rem(x + 3, 4)}, {"core": 1 - c}])
-    w = Mail(ssem, rsem)
-    ag = gather8(w, n2, n2v)
+        n1[c, x, rows, :] = (v * lax.rsqrt(jnp.mean(v * v, axis=1, keepdims=True) + EPS)).astype(BF)
+
+    keep_h = save(h, h_out)
+    n2v = n1
+    ag = gather8(w, n2v.at[c, x], n2v)
     pump([ag])
-    loads = [pltpu.make_async_copy(a, b, lsem.at[i]) for i, (a, b) in enumerate(
-        ((n2, n2v.at[c, x]), (cg, cv), (wdown, wd), (wgate, wg), (wup, wu)))]
-    for cp in loads:
-        cp.start()
-    loads[1].wait()
-    loads[2].wait()
+    pump(fl_mlp)
+    pump([ag])
+    pump([ag])
+    pump([ag])
+    pump(fl_mlp)
+    keep_cot.wait()
     down = wd[...].reshape(768, 2048)
 
     @pl.loop(0, 2)
     def _(g):
         for t in range(2):
-            dact[g, pl.ds(256 * t, 256), :] = dott(cv[g, 2 * t: 2 * t + 2].reshape(256, 2048), down)
-
-    pump([ag])
-    loads[0].wait()
-    pump([ag])
-    loads[3].wait()
-    loads[4].wait()
+            dact[g, pl.ds(256 * t, 256), :] = dott(cv[g, 2 * t: 2 * t + 2].reshape(256, 2048), down).astype(BF)
+
     gate, up = wg[...].reshape(2048, 768), wu[...].reshape(2048, 768)
     pump([ag])
 
@@ -507,7 +518,7 @@
             gp, u = dot(xv, gate), dot(xv, up)
             sig = jax.nn.sigmoid(gp)
             act = gp * sig
-            d = dact[g, rows, :]
+            d = dact[g, rows, :].astype(F32)
             a_all[g, rows, :] = (act * u).astype(BF)
             dg_all[g, rows, :] = (d * u * sig * (1.0 + gp * (1.0 - sig))).astype(BF)
             du_all[g, rows, :] = (d * act).astype(BF)
@@ -516,15 +527,28 @@
         def _(i):
             part = dott(dg_all[g], wg[i // 2, i % 2].reshape(256, 768))
             part += dott(du_all[g], wu[i // 2, i % 2].reshape(256, 768))
-            p3[g, :, :, pl.ds(pl.multiple_of(256 * i, 256), 256)] = part.astype(BF).reshape(4, 128, 256)
-
-    g0, g1 = 1 - c, c
+            p[g, :, :, pl.ds(pl.multiple_of(256 * i, 256), 256)] = part.astype(BF).reshape(4, 128, 256)
+
     st3, st2 = {}, {}
     half(g0)
-    scatter8_core(w, p3, core3, st3)
+    scatter8_core(w, p, core_r, st3)
     half(g1)
-    rs3 = scatter8_ring(w, p3, core3, hop, fin, st3)
+    rs3 = scatter8_ring(w, p, core_r, hop, fin, st3)
     pump([rs3])
+
+    at = a_all[...].reshape(1024, 768).T
+
+    @pl.loop(0, 8)
+    def _(i):
+        cols = pl.ds(pl.multiple_of(256 * i, 256), 256)
+        d_down[:, :, :, cols] = dot(at, cv[:, :, :, cols].reshape(1024, 256)).astype(BF).reshape(4, 4, 48, 256)
+
+    left, right_cols = pl.ds(0, 1024), pl.ds(1024, 1024)
+    landed = others(w, y, "y", lambda pp: d_down.at[:, pp, :, left], r1_down.at[0])
+    landed += others(w, z, "z", lambda pp: d_down.at[pp, :, :, right_cols], r1_down.at[1])
+    save(d_down, g_down)
+
+    p2 = cv
 
     def out_part(g):
         @pl.loop(0, 8)
@@ -537,18 +561,19 @@
     out_part(g1)
     pump([rs3])
 
-    dg, du, av = dg_all[...].reshape(1024, 768), du_all[...].reshape(1024, 768), a_all[...].reshape(1024, 768)
+    dg, du = dg_all[...].reshape(1024, 768), du_all[...].reshape(1024, 768)
 
     def stage(i, k):
-        return pltpu.make_async_copy(st_w.at[i % 2, k], (g_gate, g_up)[k].at[i // 2, i % 2], lsem.at[5 + 2 * (i % 2) + k])
+        rows = pl.ds(256 * k, 256)
+        return pltpu.make_async_copy(dact.at[i % 2, rows], (g_gate, g_up)[k].at[i], lsem.at[7 + 2 * (i % 2) + k])
 
     for i in range(8):
         t = n2v[:, :, :, 256 * i: 256 * i + 256].reshape(1024, 256).T
         if i >= 2:
             stage(i - 2, 0).wait()
             stage(i - 2, 1).wait()
-        st_w[i % 2, 0] = dot(t, dg).astype(BF).reshape(4, 4, 16, 768)
-        st_w[i % 2, 1] = dot(t, du).astype(BF).reshape(4, 4, 16, 768)
+        dact[i % 2, 0:256, :] = dot(t, dg).astype(BF)
+        dact[i % 2, 256:512, :] = dot(t, du).astype(BF)
         stage(i, 0).start()
         stage(i, 1).start()
 
@@ -556,61 +581,61 @@
     for i, b in enumerate((opp, right, left, x)):
         w.got(core2.at[i], st2["k"][i], to_c)
         add_to(p2.at[c, b], core2.at[i], 0, 128)
-    save = pltpu.make_async_copy(p2.at[c], s2, lsem.at[9])
-    save.start()
-    ct = cv[...].reshape(1024, 2048)
-
-    def keep(i):
-        return pltpu.make_async_copy(st_d.at[i], g_down.at[pl.ds(i, 1)], lsem.at[10 + i])
-
-    for i in range(4):
-        t = av[:, 192 * i: 192 * i + 192].T
-        st_d[i] = dot(t, ct).astype(BF).reshape(1, 4, 48, 2048)
-        keep(i).start()
+    save(p2.at[c], s2)
     pump([rs3])
+    keep_h.wait()
 
     @pl.loop(0, 8)
     def _(i):
         rows = pl.ds(pl.multiple_of(i * 16, 16), 16)
-        e = p3[c, x, rows, :].astype(F32) + core3[3, rows, :].astype(F32)
+        e = p[c, x, rows, :].astype(F32) + core_r[3, rows, :].astype(F32)
         e = e + fin[0, rows, :].astype(F32) + fin[1, rows, :].astype(F32)
         v = h[rows, :]
         r = lax.rsqrt(jnp.mean(v * v, axis=1, keepdims=True) + EPS)
         out = cot[rows, :].astype(F32) + r * e - v * (r * r * r * jnp.mean(e * v, axis=1, keepdims=True))
-        dh[rows, :] = out
-        da[rows, :] = out.astype(BF)
-
+        h[rows, :] = out
+        n1[c, x, rows, :] = out.astype(BF)
+
+    save(h, dh_out)
+    save(n1.at[c, x], da_out)
     w.drain()
-    save.wait()
     for i in (6, 7):
         stage(i, 0).wait()
         stage(i, 1).wait()
-    for i in range(4):
-        keep(i).wait()
-
-
-def feed_forward(n2, h, cot, cg, wgate, wup, wdown, cid):
+    for a in landed:
+        w.got(*a)
+    for cp in saved:
+        if all(cp is not a for a in (keep_n1, keep_h, keep_cot)):
+            cp.wait()
+
+
+def forward_layer(lens, tokens, cos, sin, cot, qkv_s, out_s, gate_s, up_s, down_s, cid):
     sds = jax.ShapeDtypeStruct
     vm, hb = pl.BlockSpec(memory_space=VMEM), pl.BlockSpec(memory_space=ANY)
-    col = (4, 2, 4, 4, 16, 768)
-    outs = [(sds((128, 2048), F32), vm), (sds((128, 2048), BF), vm), (sds((4, 128, 2048), BF), hb),
-            (sds(col, BF), hb), (sds(col, BF), hb), (sds((4, 4, 48, 2048), BF), hb)]
+    col, big = (4, 2, 4, 4, 16, 768), (2, 4, 128, 2048)
+    row = (128, 2048)
+    mid = [((2, 4, 512, 128), BF), ((2, 4, 4, 128, 128), BF), ((2, 512, 256), BF), ((2, 4, 512), F32),
+           ((4, 2, 4, 4, 16, 384), BF), ((4, 4, 16, 2048), BF)]
+    outs = [(row, F32), (big, BF)] + mid + [
+        (row, F32), (row, BF), ((4, 128, 2048), BF), ((8, 256, 768), BF), ((8, 256, 768), BF), ((4, 4, 48, 2048), BF),
+        ((2, 3, 4, 48, 1024), BF)]
+    scratch = [((2, 512, 128), F32)] * 2 + [(row, F32)] + mid + [
+        (big, BF), (big, BF), (col, BF), (col, BF), ((4, 4, 48, 2048), BF),
+        (big, BF), ((4, 128, 2048), BF), ((2, 64, 2048), BF), ((2, 128, 2048), BF),
+        ((2, 512, 768), BF), ((2, 512, 768), BF), ((2, 512, 768), BF), ((2, 512, 768), BF),
+        ((4, 128, 2048), BF), ((4, 4, 48, 2048), BF)]
     return pl.pallas_call(
-        m2_kernel,
-        out_shape=[a for a, _ in outs],
-        in_specs=[hb, vm, vm, hb, hb, hb, hb],
-        out_specs=[b for _, b in outs],
-        scratch_shapes=[
-            VMEM((2, 4, 128, 2048), BF), VMEM((2, 4, 128, 2048), BF), VMEM(col, BF), VMEM(col, BF),
-            VMEM((4, 4, 48, 2048), BF), VMEM((2, 512, 768), F32), VMEM((2, 512, 768), BF), VMEM((2, 512, 768), BF),
-            VMEM((2, 512, 768), BF), VMEM((2, 4, 128, 2048), BF), VMEM((2, 4, 128, 2048), BF),
-            VMEM((4, 128, 2048), BF), VMEM((4, 128, 2048), BF), VMEM((2, 64, 2048), BF), VMEM((2, 128, 2048), BF),
-            VMEM((2, 2, 4, 4, 16, 768), BF), VMEM((4, 1, 4, 48, 2048), BF),
-            pltpu.SemaphoreType.DMA((30,)), pltpu.SemaphoreType.DMA((30,)), pltpu.SemaphoreType.DMA((14,)),
+        forward_kernel,
+        out_shape=[sds(*a) for a in outs],
+        in_specs=[pl.BlockSpec(memory_space=pltpu.SMEM), vm, hb, hb, vm] + [hb] * 5,
+        out_specs=[hb] * len(outs),
+        scratch_shapes=[VMEM(*a) for a in scratch] + [
+            pltpu.SemaphoreType.DMA((170,)), pltpu.SemaphoreType.DMA((170,)), pltpu.SemaphoreType.DMA((13,)),
+            pltpu.SemaphoreType.DMA((16,)),
         ],
         compiler_params=comm_params(cid, 63),
-        name="feed_forward",
-    )(n2, h, cot, cg, wgate, wup, wdown)
+        name="forward_layer",
+    )(lens, tokens, cos, sin, cot, qkv_s, out_s, gate_s, up_s, down_s)
 
 
 def ring_tail(w, s, hop, fin):
@@ -679,19 +704,22 @@
     sum_four(s.at[e], piece2(q2), r2, (4,))
 
 
-def row_job(w, src, r1, t, r2, s, e, z, y, lsem):
-    n = src.shape[-1] // 2
-    rows = src.shape[2]
+def row_job(w, src, r1, t, r2, s, e, z, y, lsem, here=None):
+    n = s.shape[-1] // 2
+    rows = s.shape[0]
     cols = pl.ds(e * n, n)
+    if len(src.shape) == 5:
+        at = lambda *q: src.at[(e,) + q]
+    else:
+        at = lambda *q: src.at[q + (slice(None), cols)]
     if e == 0:
-        own, piece1, ax1, q1 = src.at[:, y, :, cols], lambda p: src.at[:, p, :, cols], "y", y
-        ax2, q2 = "z", z
+        piece1, ax1, q1, ax2, q2 = lambda p: at(slice(None), p), "y", y, "z", z
     else:
-        own, piece1, ax1, q1 = src.at[z, :, :, cols], lambda p: src.at[p, :, :, cols], "z", z
-        ax2, q2 = "y", y
+        piece1, ax1, q1, ax2, q2 = lambda p: at(p, slice(None)), "z", z, "y", y
+    own = piece1(q1)
     first = pltpu.make_async_copy(own, t, lsem)
     first.start()
-    waits = others(w, q1, ax1, piece1, r1)
+    waits = others(w, q1, ax1, piece1, r1) if here is None else []
     yield
     first.wait()
     for a in waits:
@@ -723,14 +751,14 @@
         w.got(f.at[rr], k, {"x": rr // 2, "core": lax.rem(rr, 2)})
 
 
-def m3_kernel(lens, da, dh, x_ref, h, cos, sin, n1g, wqkv, wout, qp, kv, o, lse, s2, g_gate, g_up, g_down,
-              out, gt, f_gate, f_up, f_qkv, f_down, f_out,
+def m3_kernel(lens, da, dh, x_ref, h, cos, sin, n1g, wqkv, wout, qp, kv, o, lse, s2, g_gate, g_up, g_down, r1_down,
+              out, gt, f_gate, f_up, f_q, f_kv, f_down, f_out,
               dav, n1v, s2v, do4, delta, acc, kvt, dqt, dkv_s, dkv_r, dqkv, p4, core_r, hop, fin, hop2, fin2,
-              d_qkv, d_out,
-              ra0, ra1, rb0, rb1, rc0, rc1, rd0, rd1, re0, re1,
-              ta0, ta1, tb0, tb1, tc0, tc1, td0, td1, te0, te1,
-              qa0, qa1, qb0, qb1, qc0, qc1, qd0, qd1, qe0, qe1,
-              s_gate, s_up, s_qkv, s_down, s_out, ssem, rsem, lsem):
+              d_q, d_kv, d_out,
+              ra0, ra1, rb0, rb1, rc, rd0, rd1, re0, re1, rf0, rf1,
+              ta0, ta1, tb0, tb1, tc0, tc1, td0, td1, te0, te1, tf0, tf1,
+              qa0, qa1, qb0, qb1, qc0, qc1, qd0, qd1, qe0, qe1, qf0, qf1,
+              s_gate, s_up, s_q, s_kv, s_down, s_out, ssem, rsem, lsem):
     z, c, x, y = (lax.axis_index(a) for a in ALL)
     peers = [to for _, to in tp_peers(c, x)]
     for axis, q in (("y", y), ("z", z)):
@@ -740,22 +768,27 @@
     ag = gather8(w, da, dav)
     pump([ag])
     loads = [pltpu.make_async_copy(a, b, lsem.at[i]) for i, (a, b) in enumerate(
-        ((da, dav.at[c, x]), (s2, s2v), (n1g, n1v)))]
+        ((da, dav.at[c, x]), (s2, s2v), (n1g, n1v), (r1_down, rc)))]
     for cp in loads:
         cp.start()
+    jobs_down = [
+        row_job(w, g_down, rc.at[0], tc0, qc0, s_down, 0, z, y, lsem.at[7], loads[3]),
+        row_job(w, g_down, rc.at[1], tc1, qc1, s_down, 1, z, y, lsem.at[8], loads[3]),
+    ]
     jobs = [
-        col_job(w, g_gate, ra0, ta0, qa0, s_gate, 0, z, y, lsem.at[3]),
-        col_job(w, g_gate, ra1, ta1, qa1, s_gate, 1, z, y, lsem.at[4]),
-        col_job(w, g_up, rb0, tb0, qb0, s_up, 0, z, y, lsem.at[5]),
-        col_job(w, g_up, rb1, tb1, qb1, s_up, 1, z, y, lsem.at[6]),
-        row_job(w, g_down, rc0, tc0, qc0, s_down, 0, z, y, lsem.at[7]),
-        row_job(w, g_down, rc1, tc1, qc1, s_down, 1, z, y, lsem.at[8]),
+        col_job(w, g_gate, ra0, ta0, qa0, s_gate, 0, z, y, lsem.at[4]),
+        col_job(w, g_gate, ra1, ta1, qa1, s_gate, 1, z, y, lsem.at[5]),
+        col_job(w, g_up, rb0, tb0, qb0, s_up, 0, z, y, lsem.at[6]),
+        col_job(w, g_up, rb1, tb1, qb1, s_up, 1, z, y, lsem.at[9]),
     ]
+    pump(jobs_down)
     pump(jobs)
     pump([ag])
     loads[0].wait()
     pump([ag])
+    pump([ag])
     loads[1].wait()
+    loads[3].wait()
     tail2 = ring_tail(w, s2v, hop2, fin2)
     pump([tail2])
     pump([ag])
@@ -784,8 +817,8 @@
         d_out[:, :, :, cols] = dot(ot, dav[:, :, :, cols].reshape(1024, 256)).astype(BF).reshape(4, 4, 16, 256)
 
     jobs_out = [
-        row_job(w, d_out, rd0, td0, qd0, s_out, 0, z, y, lsem.at[9]),
-        row_job(w, d_out, rd1, td1, qd1, s_out, 1, z, y, lsem.at[10]),
+        row_job(w, d_out, rd0, td0, qd0, s_out, 0, z, y, lsem.at[10]),
+        row_job(w, d_out, rd1, td1, qd1, s_out, 1, z, y, lsem.at[11]),
     ]
     pump(jobs_out)
 
@@ -818,31 +851,32 @@
             for t in range(2):
                 v = pair_heads(dq[256 * t: 256 * t + 128], dq[256 * t + 128: 256 * t + 256], True) * (HD ** -0.5)
                 dqkv[g, rows, 128 * t: 128 * t + 128] = (v * cs - swap_halves(v) * sn).astype(BF)
-            if j == 1:
-                if no == 0:
-                    pump(jobs[:2])
-                    pump([tail2])
-                    pump(jobs[2:])
-                else:
-                    pump(jobs + jobs_out)
-                    ends = [hand_out(w, s_gate, f_gate, c, x), hand_out(w, s_up, f_up, c, x),
-                            transpose_zx(w, s_down, lambda zz: f_down, z, x, lsem.at[11])]
-                    pump(ends)
+            if no == 0 and j == 2:
+                pump([tail2])
+            if no == 1 and j == 2:
+                pump(jobs_out)
         dkv_s[no] = acc[...].astype(BF).reshape(4, 4, 128, 128)
         waits[no] = others(w, y, "y", lambda p, no=no: dkv_s.at[no, :, p], dkv_r.at[no])
         if no == 0:
-            pump(jobs_out)
+            pump(jobs_down)
+            pump(jobs)
+    pump(jobs)
+    ends = [hand_out(w, s_gate, f_gate, c, x), hand_out(w, s_up, f_up, c, x)]
+    pump(ends)
     pump([tail2])
+    loads[2].wait()
+    dv = dqkv[:, :, 0:256].reshape(1024, 256)
 
     @pl.loop(0, 8)
     def _(i):
-        rows = pl.ds(pl.multiple_of(i * 16, 16), 16)
-        v = h[rows, :] + s2v[x, rows, :].astype(F32) + fin2[0, rows, :].astype(F32) + fin2[1, rows, :].astype(F32)
-        out[rows, :] = v.astype(BF)
-
-    pump(jobs_out)
-    tr_out = transpose_zx(w, s_out, lambda zz: f_out, z, x, lsem.at[12])
-    pump([tr_out])
+        cols = pl.ds(pl.multiple_of(256 * i, 256), 256)
+        d_q[i // 2, i % 2] = dot(n1v[:, :, :, cols].reshape(1024, 256).T, dv).astype(BF).reshape(4, 4, 16, 256)
+
+    jobs_q = [
+        col_job(w, d_q, re0, te0, qe0, s_q, 0, z, y, lsem.at[12]),
+        col_job(w, d_q, re1, te1, qe1, s_q, 1, z, y, lsem.at[13]),
+    ]
+    pump(jobs_q)
 
     state = {}
     for no, g in enumerate((g0, g1)):
@@ -865,24 +899,39 @@
             scatter8_core(w, p4, core_r, state)
     rs = scatter8_ring(w, p4, core_r, hop, fin, state)
     pump([rs])
-    loads[2].wait()
-    dv = dqkv[...].reshape(1024, 384)
+    dv = dqkv[:, :, 256:384].reshape(1024, 128)
 
     @pl.loop(0, 8)
     def _(i):
         cols = pl.ds(pl.multiple_of(256 * i, 256), 256)
-        d_qkv[i // 2, i % 2] = dot(n1v[:, :, :, cols].reshape(1024, 256).T, dv).astype(BF).reshape(4, 4, 16, 384)
-
-    jobs_qkv = [
-        col_job(w, d_qkv, re0, te0, qe0, s_qkv, 0, z, y, lsem.at[13]),
-        col_job(w, d_qkv, re1, te1, qe1, s_qkv, 1, z, y, lsem.at[14]),
+        d_kv[i // 2, i % 2] = dot(n1v[:, :, :, cols].reshape(1024, 256).T, dv).astype(BF).reshape(4, 4, 16, 128)
+
+    jobs_kv = [
+        col_job(w, d_kv, rf0, tf0, qf0, s_kv, 0, z, y, lsem.at[14]),
+        col_job(w, d_kv, rf1, tf1, qf1, s_kv, 1, z, y, lsem.at[15]),
     ]
-    pump(jobs_qkv)
+    pump(jobs_kv)
+
+    @pl.loop(0, 8)
+    def _(i):
+        rows = pl.ds(pl.multiple_of(i * 16, 16), 16)
+        v = h[rows, :] + s2v[x, rows, :].astype(F32) + fin2[0, rows, :].astype(F32) + fin2[1, rows, :].astype(F32)
+        out[rows, :] = v.astype(BF)
+
     pump([rs])
-    pump(jobs_qkv)
-    pump(jobs_qkv)
-    end_qkv = hand_out(w, s_qkv, f_qkv, c, x)
-    pump([end_qkv])
+    pump(jobs_out)
+    pump(jobs_q)
+    pump(jobs_kv)
+    more = [transpose_zx(w, s_out, lambda zz: f_out, z, x, lsem.at[17])]
+    pump(more)
+    pump(jobs_q)
+    pump(jobs_kv)
+    more += [hand_out(w, s_q, f_q, c, x), hand_out(w, s_kv, f_kv, c, x)]
+    pump(more[1:])
+    pump(jobs_down)
+    more += [transpose_zx(w, s_down, lambda zz: f_down, z, x, lsem.at[16])]
+    pump(more[3:])
+    ends += more
     pump([rs])
 
     @pl.loop(0, 8)
@@ -895,36 +944,41 @@
         gt[rows, :] = dh[rows, :] + r * e - v * (r * r * r * jnp.mean(e * v, axis=1, keepdims=True))
 
     pump(ends)
-    pump([tr_out, end_qkv])
     w.drain()
 
 
-def backward_attention(lens, da, dh, x, h, cos, sin, n1g, wqkv, wout, qp, kv, o, lse, s2, g_gate, g_up, g_down, cid):
+def backward_attention(
+        lens, da, dh, x, h, cos, sin, n1g, wqkv, wout, qp, kv, o, lse, s2, g_gate, g_up, g_down, r1_down, cid):
     sds = jax.ShapeDtypeStruct
     vm, hb = pl.BlockSpec(memory_space=VMEM), pl.BlockSpec(memory_space=ANY)
     outs = [sds((128, 2048), BF), sds((128, 2048), F32), sds((8, 16, 768), BF), sds((8, 16, 768), BF),
-            sds((8, 16, 384), BF), sds((48, 2048), BF), sds((16, 2048), BF)]
+            sds((8, 16, 256), BF), sds((8, 16, 128), BF), sds((48, 2048), BF), sds((16, 2048), BF)]
     b = lambda *s: VMEM(s, BF)
-    r1 = [b(3, 4, 4, 16, 768)] * 4 + [b(3, 4, 48, 1024)] * 2 + [b(3, 4, 16, 1024)] * 2 + [b(3, 4, 4, 16, 384)] * 2
-    t1 = [b(4, 4, 16, 768)] * 4 + [b(4, 48, 1024)] * 2 + [b(4, 16, 1024)] * 2 + [b(4, 4, 16, 384)] * 2
-    r2 = [b(3, 4, 16, 768)] * 4 + [b(3, 48, 1024)] * 2 + [b(3, 16, 1024)] * 2 + [b(3, 4, 16, 384)] * 2
+    ns = (768, 768, 256, 128)
+    r1 = [b(3, 4, 4, 16, 768)] * 4 + [b(2, 3, 4, 48, 1024)] + [b(3, 4, 16, 1024)] * 2
+    r1 += [b(3, 4, 4, 16, 256)] * 2 + [b(3, 4, 4, 16, 128)] * 2
+    t1 = [b(4, 4, 16, 768)] * 4 + [b(4, 48, 1024)] * 2 + [b(4, 16, 1024)] * 2
+    t1 += [b(4, 4, 16, 256)] * 2 + [b(4, 4, 16, 128)] * 2
+    r2 = [b(3, 4, 16, 768)] * 4 + [b(3, 48, 1024)] * 2 + [b(3, 16, 1024)] * 2
+    r2 += [b(3, 4, 16, 256)] * 2 + [b(3, 4, 16, 128)] * 2
     return pl.pallas_call(
         m3_kernel,
         out_shape=outs,
-        in_specs=[pl.BlockSpec(memory_space=pltpu.SMEM), hb] + [vm] * 5 + [hb] + [vm] * 6 + [hb] * 4,
-        out_specs=[vm] * 7,
+        in_specs=[pl.BlockSpec(memory_space=pltpu.SMEM), hb] + [vm] * 5 + [hb] + [vm] * 6 + [hb] * 5,
+        out_specs=[vm] * 8,
         scratch_shapes=[
             b(2, 4, 128, 2048), b(2, 4, 128, 2048), b(4, 128, 2048), b(2, 4, 512, 128), VMEM((2, 4, 512), F32),
             VMEM((4, 512, 128), F32), b(128, 2048), VMEM((128, 512), F32), b(2, 4, 4, 128, 128),
             b(2, 3, 4, 128, 128), b(2, 512, 384), b(2, 4, 128, 2048), b(4, 128, 2048), b(2, 64, 2048),
-            b(2, 128, 2048), b(2, 64, 2048), b(2, 128, 2048), b(4, 2, 4, 4, 16, 384), b(4, 4, 16, 2048),
+            b(2, 128, 2048), b(2, 64, 2048), b(2, 128, 2048),
+            b(4, 2, 4, 4, 16, 256), b(4, 2, 4, 4, 16, 128), b(4, 4, 16, 2048),
         ] + r1 + t1 + r2 + [
-            b(2, 4, 16, 768), b(2, 4, 16, 768), b(2, 4, 16, 384), b(48, 2048), b(16, 2048),
-            pltpu.SemaphoreType.DMA((130,)), pltpu.SemaphoreType.DMA((130,)), pltpu.SemaphoreType.DMA((15,)),
+            b(2, 4, 16, 768), b(2, 4, 16, 768), b(2, 4, 16, 256), b(2, 4, 16, 128), b(48, 2048), b(16, 2048),
+            pltpu.SemaphoreType.DMA((150,)), pltpu.SemaphoreType.DMA((150,)), pltpu.SemaphoreType.DMA((18,)),
         ],
         compiler_params=comm_params(cid, 63),
         name="backward_attention",
-    )(lens, da, dh, x, h, cos, sin, n1g, wqkv, wout, qp, kv, o, lse, s2, g_gate, g_up, g_down)
+    )(lens, da, dh, x, h, cos, sin, n1g, wqkv, wout, qp, kv, o, lse, s2, g_gate, g_up, g_down, r1_down)
 
 
 def local(tokens, lengths, attn_gain, w_query, w_key, w_value, w_out, mlp_gain, w_gate, w_up, w_down, cotangent):
@@ -951,17 +1005,18 @@
     angle = (place - start)[:, :, None].astype(F32) * frequency
     cos, sin = jnp.cos(angle), jnp.sin(angle) * sign
 
-    h, n2, n1g, cg, qp, kv, o, lse, wqkv, wout, wgate, wup, wdown = forward_attention(
+    h, n1g, qp, kv, o, lse, wqkv, wout, dh, da, s2, g_gate, g_up, g_down, r1_down = forward_layer(
         lens, tokens, cos, sin, cotangent, qkv_s, w_out, gate_s, up_s, down_s, 1)
-    dh, da, s2, g_gate, g_up, g_down = feed_forward(n2, h, cotangent, cg, wgate, wup, wdown, 2)
-    output, grad_tokens, gate_s, up_s, qkv_s, down_s, out_s = backward_attention(
-        lens, da, dh, tokens, h, cos, sin, n1g, wqkv, wout, qp, kv, o, lse, s2, g_gate, g_up, g_down, 3)
+    col = (4, 2, 4, 4, 16, 768)
+    g_gate, g_up = g_gate.reshape(col), g_up.reshape(col)
+    output, grad_tokens, gate_s, up_s, q_s, kv_s, down_s, out_s = backward_attention(
+        lens, da, dh, tokens, h, cos, sin, n1g, wqkv, wout, qp, kv, o, lse, s2, g_gate, g_up, g_down, r1_down, 3)
 
     wide = lambda v: v.astype(F32).transpose(1, 0, 2).reshape(16, -1)
     unpad = lambda v: v.reshape(16, 128, 48)[:, :, :44].reshape(16, 5632)
     g_gate, g_up = unpad(wide(gate_s)), unpad(wide(up_s))
     pair = lambda v: v.astype(F32).reshape(4, 2, 16, HD).sum(axis=1).transpose(1, 0, 2).reshape(16, -1)
-    g_query, g_key, g_value = wide(qkv_s[..., :256]), pair(qkv_s[..., 256:320]), pair(qkv_s[..., 320:])
+    g_query, g_key, g_value = wide(q_s), pair(kv_s[..., :64]), pair(kv_s[..., 64:])
     rowdot = lambda w, gr: jnp.sum(w.astype(F32) * gr, axis=1)
     grad_attn_gain = rowdot(w_query, g_query) + rowdot(w_key, g_key) + rowdot(w_value, g_value)
     grad_mlp_gain = rowdot(w_gate, g_gate) + rowdot(w_up, g_up)

time: 374 us -> 309 us (0.83)
  Pallas kernels: 334 us -> 268 us
    pallas_call x2 -> x1, Pallas kernels: 203 us -> 156 us  [forward_layer(): pl.pallas_call(forward_kernel, out_shape=[sds(*a) for a in outs], in_spec...]
    pallas_call x1, Pallas kernels: 131 us -> 112 us  [backward_attention(): pl.pallas_call(m3_kernel, out_shape=outs, in_specs=[pl.BlockSpec(memory_s...]
where the time goes in v2:
time: 309 us; the launch traced here: 304 us
  Pallas kernels  268 us (87%)
  other arithmetic  16.9 us (5%)
  local copies, waits for them, and re-layouts  14.9 us (5%)
    pallas_call x1, Pallas kernels, forward_layer(): pl.pallas_call(forward_kernel, out_shape=[sds(*a) for a in outs], in_spec...  156 us
    pallas_call x1, Pallas kernels, backward_attention(): pl.pallas_call(m3_kernel, out_shape=outs, in_specs=[pl.BlockSpec(memory_s...  112 us

profile of v2, /device:TPU:1, one launch (start us, length us, event | category | flops | bytes accessed | tf_op | source)
XLA Modules:
  0.0 303.7 jit_solution(13446871336507863899)
XLA Ops:
  0.7 0.7 convert_element_type.75
  1.3 0.7 convert_element_type.82
  2.0 3.0 all-gather
  5.0 0.1 add_bitcast_fusion
  5.1 0.2 fusion.16
  5.2 0.6 pad_add_fusion.lens
  5.9 0.1 fusion.12
  6.0 0.8 fusion.7
  6.8 0.1 reshape.248
  6.9 0.1 reshape.250
  7.0 0.9 fusion.5
  7.9 0.7 maximum_bitcast_fusion.qkv_s
  8.6 1.6 pad.13.down_s
  10.3 1.1 fusion.3
  11.4 1.5 reshape.254
  12.9 0.1 pad.12
  13.0 1.1 reshape.255
  14.2 1.5 reshape.252
  15.7 0.1 pad.11
  15.9 1.2 reshape.253
  17.0 3.0 fusion
  20.0 155.6 %forward_layer.1 = (f32[128,2048]{1,0:T(8,128)}, bf16[2,4,128,2048]{3,2,1,0:T(8,128)(2,1)}, bf16[2,4,512,128]{3,2,1,0:T(8,128)(2,1)}, bf16[2,4,4,128,128]{4,3,2,...) custom-call(s32[2,2]{1,0:T(2,128)} %pad_add_fusion.lens, ...), custom_call_target="tpu_custom_call" | custom-call | tf_op jit(solution)/shard_map/forward_layer/pallas_call | solution.py:627
  175.6 0.0 copy-start.5
  175.7 0.0 copy-start.6
  175.7 0.0 copy-start.3
  175.7 112.1 %backward_attention.1 = (bf16[128,2048]{1,0:T(8,128)(2,1)}, f32[128,2048]{1,0:T(8,128)}, bf16[8,16,768]{2,1,0:T(8,128)(2,1)}, bf16[8,16,768]{2,1,0:T(8,128)(2,1)...) custom-call(s32[2,2]{1,0:T(2,128)} %pad_add_fusion.lens, ...), custom_call_target="tpu_custom_call" | custom-call | tf_op jit(solution)/shard_map/backward_attention/pallas_call | solution.py:964
  287.8 0.0 copy-start.4
  287.8 0.9 convert_reduce_fusion.1
  288.8 0.1 reshape.262
  288.9 0.1 reshape.265
  289.0 0.0 copy-done.5
  289.0 0.0 copy-done.6
  289.0 0.8 broadcast_multiply_fusion.3
  289.8 0.9 convert_bitcast_fusion
  290.7 0.0 copy-done.3
  290.7 0.8 broadcast_multiply_fusion.2
  291.5 0.5 add_add_fusion
  292.0 1.5 convert_element_type.86
  293.5 1.0 copy.51
  294.5 1.0 copy.52
  295.5 0.6 reshape_reshape.9
  296.2 0.6 reshape_reshape.8
  296.8 0.0 copy-done.4
  296.8 0.0 copy-start.1
  296.8 0.0 copy-start.2
  296.8 0.8 slice_convert_fusion.2
  297.6 0.1 slice_convert_fusion.1
  297.7 0.6 reshape.277
  298.3 0.0 copy-start
  298.3 0.1 slice_convert_fusion
  298.4 0.6 reshape.279
  299.0 0.0 copy-done.1
  299.0 0.0 copy-done.2
  299.0 1.1 broadcast_multiply_fusion
  300.1 0.5 add.81
  300.6 1.9 copy.59
  302.5 0.0 copy-done
  302.5 1.0 copy.60
  (12 shorter events, 0.2 us)
Async XLA Ops:
  175.6 113.3 %copy-start.5 = (bf16[16,256]{1,0:T(8,128)(2,1)S(1)}, bf16[16,256]{1,0:T(8,128)(2,1)}, u32[]{:S(2)}) copy-start(bf16[16,256]{1,0:T(8,128)(2,1)} %param.16) | copy-start | bytes 24580
  175.7 113.3 %copy-start.6 = (bf16[16,256]{1,0:T(8,128)(2,1)S(1)}, bf16[16,256]{1,0:T(8,128)(2,1)}, u32[]{:S(2)}) copy-start(bf16[16,256]{1,0:T(8,128)(2,1)} %param.17) | copy-start | bytes 24580
  175.7 115.0 %copy-start.3 = (bf16[16,2048]{1,0:T(8,128)(2,1)S(1)}, bf16[16,2048]{1,0:T(8,128)(2,1)}, u32[]{:S(2)}) copy-start(bf16[16,2048]{1,0:T(8,128)(2,1)} %param.15) | copy-start | bytes 196612
  287.8 9.0 %copy-start.4 = (bf16[48,2048]{1,0:T(8,128)(2,1)S(1)}, bf16[48,2048]{1,0:T(8,128)(2,1)}, u32[]{:S(2)}) copy-start(bf16[48,2048]{1,0:T(8,128)(2,1)} %get-tuple-element.56) | copy-start | bytes 589828
  296.8 2.2 copy-start.1
  296.8 2.2 copy-start.2
  298.3 4.2 %copy-start = (f32[128,2048]{1,0:T(8,128)S(1)}, f32[128,2048]{1,0:T(8,128)}, u32[]{:S(2)}) copy-start(f32[128,2048]{1,0:T(8,128)} %get-tuple-element.97) | copy-start | bytes 3145732
